TPU v7x, 128 devices: a whole 4x4x4 slice. The times are simulated.
128 devices in a mesh: tgt: 2 (over z_hi), fsdp: 16 (over z_lo, x, core), dp: 4 (over y).
Axes of the slice: x: 4, y: 4, z: 4 (z_hi: 2, z_lo: 2; z = z_hi * 2 + z_lo), core: 2. Of those that a mesh axis runs over, the one named last changes fastest.
Arguments:
- tokens: bfloat16 [49152, 1408], P(('tgt', 'fsdp', 'dp')), may hold values from -6 to 6
- widen_weight: bfloat16 [1408, 6144], P(None, 'fsdp'), may hold values from -0.15625 to 0.15625
- narrow_weight: bfloat16 [6144, 1408], P(None, 'fsdp'), may hold values from -0.078125 to 0.078125
- head_weight: bfloat16 [384, 1408], P(None, 'fsdp'), may hold values from -0.3125 to 0.3125
- predictor_rows: bfloat16 [131072, 384], P(('tgt', 'fsdp', 'dp')), may hold values from -24 to 24
- target_index: int32 [32768], P(('tgt', 'fsdp', 'dp')), may hold values from 0 to 383, as said below
- destination: int32 [32768, 1], P(('tgt', 'fsdp', 'dp')), may hold values from 0 to 31; in each aligned block of 256 rows (0 to 255, 256 to 511, ...) at most 32 rows name the same one
Outputs:
- target_features: bfloat16 [49152, 1408], P(('tgt', 'fsdp', 'dp'))
- target_error: bfloat16 [131072, 1408], P(('tgt', 'fsdp', 'dp'))
- head_gradient: float32 [384, 1408], P('fsdp')
Inputs may be any that keep to these rules, and one draw needn't show every extreme that they name: `target_index`: each block of 256 entries lists distinct rows of its device, in rising order. `destination`: among the 256 rows of one device no owner is named more than 32 times, a bound that some block reaches.
All inputs are finite; a program needn't handle non-finite values.
Results may differ from a plain program's by a relative error of at most 0.015.
Values may be sent and summed in bfloat16 or wider, within the bound.
A program may use at most 128 MiB of HBM per device.

v0:
```python
import math

import jax
import jax.numpy as jnp
from jax import lax
from jax.sharding import PartitionSpec as P


def norm_rows(values):
    center = jnp.mean(values, axis=-1, keepdims=True)
    shifted = values - center
    spread = jnp.mean(shifted * shifted, axis=-1, keepdims=True)
    return shifted * lax.rsqrt(spread + 1e-06)


def body(
    tokens, widen_weight, narrow_weight, head_weight, predictor_rows, target_index, destination
):
    owners = lax.axis_size("tgt") * lax.axis_size("fsdp")
    devices = owners * lax.axis_size("dp")
    normed = norm_rows(tokens.astype(jnp.float32)).astype(jnp.bfloat16)
    hidden = jax.nn.gelu(
        jnp.dot(
            normed,
            lax.all_gather(widen_weight, "fsdp", axis=1, tiled=True),
            preferred_element_type=jnp.float32,
        ),
        approximate=False,
    ).astype(jnp.bfloat16)
    branch = jnp.dot(
        hidden,
        lax.all_gather(narrow_weight, "fsdp", axis=1, tiled=True),
        preferred_element_type=jnp.float32,
    )
    summed = tokens.astype(jnp.float32) + branch
    features = norm_rows(summed).astype(jnp.bfloat16)
    capacity = predictor_rows.shape[0] // owners
    width_model = features.shape[1]
    picked = jnp.take(features, target_index, axis=0)
    routed = destination[:, 0]
    onehot = (routed[:, None] == jnp.arange(owners, dtype=jnp.int32)[None, :]).astype(jnp.int32)
    before = jnp.cumsum(onehot, axis=0) - onehot
    slots = jnp.sum(before * onehot, axis=1)
    position = routed * capacity + slots
    buffer = jnp.zeros((owners * capacity, width_model), jnp.bfloat16).at[position].set(picked)
    counts = jnp.sum(onehot, axis=0).astype(jnp.float32).astype(jnp.bfloat16)
    arrived, arrived_counts = (
        lax.all_to_all(
            buffer.reshape(owners, capacity, width_model),
            ("tgt", "fsdp"),
            split_axis=0,
            concat_axis=0,
            tiled=True,
        ),
        lax.all_to_all(
            counts.reshape(owners, 1), ("tgt", "fsdp"), split_axis=0, concat_axis=0, tiled=True
        ),
    )
    slot_number = jnp.arange(capacity, dtype=jnp.float32)[None, :]
    filled = (
        (slot_number < arrived_counts.astype(jnp.float32))
        .astype(jnp.float32)
        .reshape(owners * capacity, 1)
    )
    received = arrived.reshape(owners * capacity, width_model)
    prediction = jnp.dot(
        predictor_rows,
        lax.all_gather(head_weight, "fsdp", axis=1, tiled=True),
        preferred_element_type=jnp.float32,
    )
    mismatch = (filled * (prediction - received.astype(jnp.float32))).astype(jnp.bfloat16)
    shared = lax.psum_scatter(
        lax.dot_general(
            predictor_rows, mismatch, (((0,), (0,)), ((), ())), preferred_element_type=jnp.float32
        ).astype(jnp.bfloat16),
        "fsdp",
        scatter_dimension=0,
        tiled=True,
    )
    gathered_total = lax.psum(shared, ("tgt", "dp")).astype(jnp.float32)
    factor = 1.0 / math.sqrt(target_index.shape[0] * devices)
    return (features, mismatch, gathered_total * factor)


def solution(mesh):
    in_specs = (
        P(("tgt", "fsdp", "dp"), None),
        P(None, "fsdp"),
        P(None, "fsdp"),
        P(None, "fsdp"),
        P(("tgt", "fsdp", "dp"), None),
        P(("tgt", "fsdp", "dp")),
        P(("tgt", "fsdp", "dp"), None),
    )
    out_specs = (P(("tgt", "fsdp", "dp"), None), P(("tgt", "fsdp", "dp"), None), P("fsdp", None))
    return jax.shard_map(body, mesh=mesh, in_specs=in_specs, out_specs=out_specs, check_vma=False)
```

profile of v0, /device:TPU:1, one launch (start us, length us, event | category | flops | bytes accessed | tf_op | source)
XLA Modules:
  0.0 499.0 jit_solution(13575505830375024003)
XLA Ops:
  8.0 0.7 all-gather.6.cloned.1.call-update
  8.7 0.7 fusion.32
  10.2 0.9 convert_reduce_fusion.1
  11.0 0.7 copy.16
  11.8 9.4 %all-to-all-start = ((bf16[32,1,1]{2,1,0:T(2,128)(2,1)}), bf16[32,1,1]{2,1,0:T(2,128)(2,1)S(1)}, u32[]{:S(2)}, u32[]{:S(2)}) async-start(bf16[32,1,1]{2,1,0:T(2,128)(2,1)} %copy.16), calls=%async_computation | async-start | bytes 32768 | tf_op jit(solution)/shard_map/all_to_all | solution.py:55
  21.2 0.7 compare_select_fusion.1
  21.9 1.8 convert_reduce_fusion
  23.7 1.7 fusion.19
  25.3 0.7 compare_and_fusion
  26.7 80.8 %all-gather.4.cloned.1.call-done = bf16[1408,6144]{1,0:T(8,128)(2,1)} async-done(((bf16[1408,384]{1,0:T(8,128)(2,1)}), bf16[1408,6144]{1,0:T(8,128)(2,1)}) %all-gather.4.cloned.1.call-update) | async-done | bytes 17301520 | tf_op jit(solution)/shard_map/all_gather | solution.py:25
  107.5 30.6 %fusion.15.clone.4 = bf16[384,6144]{1,0:T(8,128)(2,1)} fusion(bf16[1408,6144]{1,0:T(8,128)(2,1)} %all-gather.4.cloned.1.call-done, bf16[384,1408]{1,0:T(8,128)(2,1)} %param.7, f32[384]{0:T(512)S(1)} %add_rsqrt_fusion.1, f32[384]{0:T(512)S(1)} %broadcast_multiply_fusion.1), kind=kOutput, calls=%fused_computation.5.clone.clone.clone.clone.clone.clone.1 | convolution fusion | flops 6799294464 | bytes 23104512 | tf_op jit(solution)/shard_map/dot_general | solution.py:23
  138.2 66.0 %all-gather.6.cloned.1.call-done = bf16[6144,1408]{0,1:T(8,128)(2,1)} async-done(((bf16[6144,88]{0,1:T(8,128)(2,1)}), bf16[6144,1408]{0,1:T(8,128)(2,1)}) %all-gather.6.cloned.1.call-update) | async-done | bytes 17301520 | tf_op jit(solution)/shard_map/all_gather | solution.py:32
  204.1 13.2 %fusion.65 = (f32[384]{0:T(512)S(1)}, f32[384,1408]{1,0:T(8,128)S(1)}) fusion(bf16[6144,1408]{0,1:T(8,128)(2,1)} %all-gather.6.cloned.1.call-done, bf16[384,1408]{1,0:T(8,128)(2,1)S(1)} %copy-done.1, bf16[384,6144]{1,0:T(8,128)(2,1)} %fusion.15.clone.4), kind=kOutput, calls=%fused_computation.99 | convolution fusion | flops 6645399040 | bytes 25265664 | tf_op jit(solution)/shard_map/dot_general | solution.py:30
  218.0 6.3 %scatter_custom_fusion = bf16[1024,1408]{1,0:T(8,128)(2,1)} fusion(s32[256]{0:T(256)S(1)} %bitcast.44, bf16[]{:T(256)} %constant.92.clone.1, pred[256]{0:T(512)(128)(4,1)S(1)} %compare_and_fusion, bf16[]{:T(256)} %constant.97.clone.1, bf16[384,1408]{1,0:T(8,128)(2,1)S(1)} %multiply_convert_fusion, s32[1024]{0:T(1024)S(1)} %pad_clamp_fusion), kind=kCustom, calls=%fused_computation.36 | custom fusion | flops 360448 | bytes 3969540 | tf_op jit(solution)/shard_map/scatter | solution.py:45
  224.3 6.7 %all-to-all-start.1 = ((bf16[32,32,1408]{2,1,0:T(8,128)(2,1)}), bf16[32,32,1408]{2,1,0:T(8,128)(2,1)}, u32[]{:S(2)}, u32[]{:S(2)}) async-start(bf16[32,32,1408]{2,1,0:T(8,128)(2,1)} %bitcast.40), calls=%async_computation.1 | async-start | bytes 5767168 | tf_op jit(solution)/shard_map/all_to_all | solution.py:48
  232.3 46.4 %all-gather.8.cloned.1.call-done = bf16[384,1408]{0,1:T(8,128)(2,1)} async-done(((bf16[384,88]{0,1:T(8,128)(2,1)}), bf16[384,1408]{0,1:T(8,128)(2,1)}) %all-gather.8.cloned.1.call-update) | async-done | bytes 1081360 | tf_op jit(solution)/shard_map/all_gather | solution.py:68
  278.7 3.9 fusion.11
  282.6 1.6 copy-done.3
  284.2 2.7 fusion.16
  288.2 116.3 %all-reduce.6.cloned.1.call-done = bf16[384,1408]{0,1:T(8,128)(2,1)} async-done(((bf16[384,1408]{0,1:T(8,128)(2,1)}), bf16[384,1408]{0,1:T(8,128)(2,1)}) %all-reduce.6.cloned.1.call-update) | async-done | bytes 1081360
  404.5 2.0 constant_dynamic-slice_fusion
  406.5 84.0 %all-reduce.4.cloned.1.call-done = bf16[24,1408]{0,1:T(8,128)(2,1)} async-done(((bf16[24,1408]{0,1:T(8,128)(2,1)}), bf16[24,1408]{0,1:T(8,128)(2,1)}) %all-reduce.4.cloned.1.call-update) | async-done | bytes 67600 | tf_op jit(solution)/shard_map/psum | solution.py:80
  490.6 1.0 convert_multiply_fusion
  491.6 0.9 copy.18
  (37 shorter events, 4.9 us)
Async XLA Ops:
  7.2 271.5 %copy-start = (bf16[1024,384]{1,0:T(8,128)(2,1)S(1)}, bf16[1024,384]{1,0:T(8,128)(2,1)}, u32[]{:S(2)}) copy-start(bf16[1024,384]{1,0:T(8,128)(2,1)} %param.11) | copy-start | bytes 2359300
  7.2 100.4 %all-gather.4.cloned.1.call-start = ((), (), s32[]{:S(2)}) async-start(), calls=%async_computation.2 | async-start | bytes 18382848 | tf_op jit(solution)/shard_map/all_gather | solution.py:25
  7.9 196.2 %all-gather.6.cloned.1.call-start = ((), (), s32[]{:S(2)}) async-start(), calls=%async_computation.3 | async-start | bytes 18382848 | tf_op jit(solution)/shard_map/all_gather | solution.py:32
  11.8 212.5 %all-to-all-start = ((bf16[32,1,1]{2,1,0:T(2,128)(2,1)}), bf16[32,1,1]{2,1,0:T(2,128)(2,1)S(1)}, u32[]{:S(2)}, u32[]{:S(2)}) async-start(bf16[32,1,1]{2,1,0:T(2,128)(2,1)} %copy.16), calls=%async_computation | async-start | bytes 32768 | tf_op jit(solution)/shard_map/all_to_all | solution.py:55
  26.7 177.4 %copy-start.1 = (bf16[384,1408]{1,0:T(8,128)(2,1)S(1)}, bf16[384,1408]{1,0:T(8,128)(2,1)}, u32[]{:S(2)}) copy-start(bf16[384,1408]{1,0:T(8,128)(2,1)} %param.7) | copy-start | bytes 3244036
  218.0 68.9 %copy-start.2 = (bf16[384,1408]{1,0:T(8,128)(2,1)}, bf16[384,1408]{1,0:T(8,128)(2,1)S(1)}, u32[]{:S(2)}) copy-start(bf16[384,1408]{1,0:T(8,128)(2,1)S(1)} %multiply_convert_fusion) | copy-start | bytes 3244036
  224.3 54.4 %all-to-all-start.1 = ((bf16[32,32,1408]{2,1,0:T(8,128)(2,1)}), bf16[32,32,1408]{2,1,0:T(8,128)(2,1)}, u32[]{:S(2)}, u32[]{:S(2)}) async-start(bf16[32,32,1408]{2,1,0:T(8,128)(2,1)} %bitcast.40), calls=%async_computation.1 | async-start | bytes 5767168 | tf_op jit(solution)/shard_map/all_to_all | solution.py:48
  231.0 55.9 %copy-start.4 = (u32[128]{0:T(128)S(1)}, u32[128]{0:T(128)}, u32[]{:S(2)}) copy-start(u32[128]{0:T(128)} %constant.103) | copy-start | bytes 1540
  231.0 47.6 %all-gather.8.cloned.1.call-start = ((), (), s32[]{:S(2)}) async-start(), calls=%async_computation.4 | async-start | bytes 1148928 | tf_op jit(solution)/shard_map/all_gather | solution.py:68
  231.8 172.7 %all-reduce.6.cloned.1.call-start = ((), (), s32[]{:S(2)}) async-start(), calls=%async_computation.6 | async-start | bytes 2162688
  282.6 1.6 copy-start.3
  286.9 203.6 %all-reduce.4.cloned.1.call-start = ((), (), s32[]{:S(2)}) async-start(), calls=%async_computation.5 | async-start | bytes 720896 | tf_op jit(solution)/shard_map/psum | solution.py:80
Sparse Core Ops, SparseCore 0:
  9.7 97.8 all-gather.3
  109.2 94.8 all-gather.5
  233.6 45.0 all-gather.7
  287.0 117.4 all-reduce.5
  406.8 83.6 all-reduce.3
where the time goes:
time: 504 us; the launch traced here: 499 us
  waiting for transfers between devices  396 us (79%)
  matrix products  50.4 us (10%)
  starting transfers between devices  16.4 us (3%)
  other arithmetic  16 us (3%)
  between operations  14.5 us (3%)
  local copies, waits for them, and re-layouts  6.07 us (1%)
    unnamed x6, waiting for transfers between devices  118 us
    psum x1, waiting for transfers between devices, body(): gathered_total = lax.psum(shared, ('tgt', 'dp')).astype(jnp.float32)  84 us
    all_gather x1, waiting for transfers between devices, body(): lax.all_gather(widen_weight, 'fsdp', axis=1, tiled=True)  80.8 us
    all_gather x1, waiting for transfers between devices, body(): lax.all_gather(narrow_weight, 'fsdp', axis=1, tiled=True)  66 us
    all_gather x1, waiting for transfers between devices, body(): lax.all_gather(head_weight, 'fsdp', axis=1, tiled=True)  46.4 us
    dot_general x1, matrix products, body(): jnp.dot(normed, lax.all_gather(widen_weight, 'fsdp', axis=1, tiled=True),...  30.6 us
    dot_general x1, matrix products, body(): jnp.dot(hidden, lax.all_gather(narrow_weight, 'fsdp', axis=1, tiled=True)...  13.2 us
  transfers between devices with their start and end apart: 7, of which 5 were waited for; matrix products, arithmetic and copies ran while one was open for 12% of the time, Pallas kernels for 0%

commit v1 on v0

v1 whole, which is shorter than its diff:
```python
import functools
import math

import jax
import jax.numpy as jnp
from jax import lax
from jax.experimental import pallas as pl
from jax.experimental.pallas import tpu as pltpu
from jax.sharding import PartitionSpec as P

MESH = pl.DeviceIdType.MESH
F32, BF16 = jnp.float32, jnp.bfloat16


def norm_rows(values):
    center = jnp.mean(values, axis=-1, keepdims=True)
    shifted = values - center
    spread = jnp.mean(shifted * shifted, axis=-1, keepdims=True)
    return shifted * lax.rsqrt(spread + 1e-06)


def place():
    t, f, d = lax.axis_index("tgt"), lax.axis_index("fsdp"), lax.axis_index("dp")
    return lax.rem(f // 2, 4), d, 2 * t + f // 8, lax.rem(f, 2)


def device(x, y, z, c):
    return (z // 2, lax.rem(z, 2) * 8 + x * 2 + c, y)


def send(src, dst, send_sem, recv_sem, target):
    copy = pltpu.make_async_remote_copy(src, dst, send_sem, recv_sem, device_id=target, device_id_type=MESH)
    copy.start()


def wait_recv(dst, sem, target):
    pltpu.make_async_remote_copy(dst, dst, sem, sem, device_id=target, device_id_type=MESH).wait_recv()


def wait_send(src, sem, target):
    pltpu.make_async_remote_copy(src, src, sem, sem, device_id=target, device_id_type=MESH).wait_send()


def route_kernel(
    factor, cap, feat, tokpos, counts, rows, head, error, grad,
    buf, rcv, pred, flags, flags_in, gsum, gpad, pair_in, shares, r1, r2, fin, fin_in,
    s_a, r_a, s_f, r_f, s_0, r_0, s_1, r_1, s_2, r_2, s_3, r_3,
):
    x, y, z, c = place()
    t, zl = z // 2, lax.rem(z, 2)
    me = 8 * z + 2 * x + c
    owners = 32

    def plane(r):
        nx, nz, nc = lax.rem(x + lax.rem(r // 2, 4), 4), lax.rem(z + r // 8, 4), lax.rem(c + lax.rem(r, 2), 2)
        return device(nx, y, nz, nc), 8 * nz + 2 * nx + nc

    def plane_from(r):
        nx = lax.rem(x + 4 - lax.rem(r // 2, 4), 4)
        nz, nc = lax.rem(z + 4 - r // 8, 4), lax.rem(c + lax.rem(r, 2), 2)
        return device(nx, y, nz, nc), 8 * nz + 2 * nx + nc

    def group(j):
        nt, nd = lax.rem(t + j // 4, 2), lax.rem(y + lax.rem(j, 4), 4)
        return device(x, nd, 2 * nt + zl, c), nt * 4 + nd

    def chip(j):
        nz, nx = lax.rem(zl + j // 4, 2), lax.rem(x + lax.rem(j, 4), 4)
        return device(nx, y, 2 * t + nz, c), 4 * nz + nx

    partner = device(x, y, z, 1 - c)

    barrier = pltpu.get_barrier_semaphore()

    def greet(r, _):
        pl.semaphore_signal(barrier, inc=1, device_id=plane(r)[0], device_id_type=MESH)
        return 0

    lax.fori_loop(1, owners, greet, 0)

    def greet_group(j, _):
        @pl.when(lax.rem(j, 4) != 0)
        def _():
            pl.semaphore_signal(barrier, inc=1, device_id=group(j)[0], device_id_type=MESH)

        return 0

    lax.fori_loop(1, 8, greet_group, 0)

    slot_row = lax.broadcasted_iota(jnp.int32, (cap, 128), 0)
    flags[...] = jnp.where(slot_row < counts[...], 1.0, 0.0).astype(BF16)

    def fill(i, _):
        rows_at = pl.ds(pl.multiple_of(i * 128, 128), 128)
        slot = lax.broadcasted_iota(jnp.int32, (128, feat.shape[0]), 0) + i * 128
        pick = jnp.where(slot == tokpos[...], 1.0, 0.0).astype(BF16)
        buf[rows_at, :] = jnp.dot(pick, feat[...], preferred_element_type=F32).astype(BF16)
        return 0

    lax.fori_loop(0, owners * cap // 128, fill, 0)

    pl.semaphore_wait(barrier, owners - 1 + 6)

    def out(r, _):
        target, o = plane(r)
        send(flags, flags_in.at[me], s_f.at[o], r_f.at[me], target)
        src = buf.at[pl.ds(pl.multiple_of(o * cap, cap), cap)]
        send(src, rcv.at[pl.ds(pl.multiple_of(me * cap, cap), cap)], s_a.at[o], r_a.at[me], target)
        return 0

    lax.fori_loop(1, owners, out, 0)
    mine = pl.ds(pl.multiple_of(me * cap, cap), cap)
    rcv[mine, :] = buf[mine, :]
    flags_in[me] = flags[...]

    def predict(i, _):
        rows_at = pl.ds(pl.multiple_of(i * 128, 128), 128)
        pred[rows_at, :] = jnp.dot(rows[rows_at, :], head[...], preferred_element_type=F32)
        return 0

    lax.fori_loop(0, owners * cap // 128, predict, 0)
    gsum[...] = jnp.zeros_like(gsum)

    per = 8

    def arrive(k, _):
        i = lax.rem(z + k, 4)

        def one(q, _):
            s = i * per + q

            @pl.when(s != me)
            def _():
                wait_recv(flags_in.at[s], r_f.at[s], partner)
                wait_recv(rcv.at[pl.ds(pl.multiple_of(s * cap, cap), cap)], r_a.at[s], partner)

            return 0

        lax.fori_loop(0, per, one, 0)
        rows_at = pl.ds(pl.multiple_of(i * (per * cap), per * cap), per * cap)
        lane = lax.broadcasted_iota(jnp.int32, (per * cap, 128), 1)
        live = flags_in[pl.ds(i * per, per)].astype(F32).reshape(per * cap, 128)
        live = jnp.sum(jnp.where(lane == me, live, 0.0), axis=1, keepdims=True)
        wrong = jnp.where(live > 0.5, pred[rows_at, :] - rcv[rows_at, :].astype(F32), 0.0).astype(BF16)
        error[rows_at, :] = wrong
        gsum[...] += lax.dot_general(
            rows[rows_at, :], wrong, (((0,), (0,)), ((), ())), preferred_element_type=F32
        )
        return 0

    lax.fori_loop(0, 4, arrive, 0)

    wide = gsum.shape[1]
    half = gpad.shape[1] // 2
    gpad[:, :wide] = gsum[...].astype(BF16)
    gpad[:, wide:] = jnp.zeros((gpad.shape[0], 2 * half - wide), BF16)
    theirs = pl.ds(pl.multiple_of((1 - c) * half, half), half)
    ours = pl.ds(pl.multiple_of(c * half, half), half)
    send(gpad.at[:, theirs], pair_in, s_0, r_0, partner)
    wait_recv(pair_in, r_0, partner)
    shares[...] = (gpad[:, ours].astype(F32) + pair_in[...].astype(F32)).astype(BF16)

    block = 48

    def share(j, _):
        target, b = chip(j)
        send(shares.at[pl.ds(pl.multiple_of(b * block, 16), block)], r1.at[j], s_1.at[j], r_1.at[j], target)
        return 0

    lax.fori_loop(1, 8, share, 0)
    own = shares[pl.ds(pl.multiple_of((4 * zl + x) * block, 16), block), :].astype(F32)

    def take(j, total):
        wait_recv(r1.at[j], r_1.at[j], partner)
        return total + r1[j].astype(F32)

    own = lax.fori_loop(1, 8, take, own)
    mine_at = t * 4 + y
    r2[mine_at] = own.astype(BF16)

    def spread(j, _):
        target, b = group(j)
        send(r2.at[mine_at], r2.at[mine_at], s_2.at[b], r_2.at[mine_at], target)
        return 0

    lax.fori_loop(1, 8, spread, 0)

    def settle(b, _):
        @pl.when(b != mine_at)
        def _():
            wait_recv(r2.at[b], r_2.at[b], partner)

        return 0

    lax.fori_loop(0, 8, settle, 0)

    def add(b, total):
        return total + r2[b].astype(F32)

    fin[...] = lax.fori_loop(0, 8, add, jnp.zeros(fin.shape, F32)) * factor
    send(fin, fin_in, s_3, r_3, partner)
    wait_recv(fin_in, r_3, partner)

    @pl.when(c == 0)
    def _():
        grad[:, :half] = fin[:24, :]
        grad[:, half:] = fin_in[:24, : wide - half]

    @pl.when(c == 1)
    def _():
        grad[:, :half] = fin_in[24:, :]
        grad[:, half:] = fin[24:, : wide - half]

    def done(r, _):
        o = plane(r)[1]
        wait_send(flags, s_f.at[o], partner)
        wait_send(buf.at[pl.ds(pl.multiple_of(o * cap, cap), cap)], s_a.at[o], partner)
        return 0

    lax.fori_loop(1, owners, done, 0)

    def done_shares(j, _):
        target, b = chip(j)
        wait_send(shares.at[pl.ds(pl.multiple_of(b * block, 16), block)], s_1.at[j], partner)
        wait_send(r2.at[mine_at], s_2.at[group(j)[1]], partner)
        return 0

    lax.fori_loop(1, 8, done_shares, 0)
    wait_send(gpad.at[:, theirs], s_0, partner)
    wait_send(fin, s_3, partner)


def route(features, tokpos, counts, rows, head, factor, grad_rows):
    slots, width = rows.shape[0], features.shape[1]
    cap = slots // 32
    depth = rows.shape[1]
    half = 768
    dma = pltpu.SemaphoreType.DMA
    vmem = pl.BlockSpec(memory_space=pltpu.VMEM)
    return pl.pallas_call(
        functools.partial(route_kernel, factor, cap),
        out_shape=(
            jax.ShapeDtypeStruct((slots, width), BF16),
            jax.ShapeDtypeStruct((grad_rows, width), F32),
        ),
        in_specs=[vmem] * 5,
        out_specs=(vmem, vmem),
        scratch_shapes=[
            pltpu.VMEM((slots, width), BF16),
            pltpu.VMEM((slots, width), BF16),
            pltpu.VMEM((slots, width), F32),
            pltpu.VMEM((cap, 128), BF16),
            pltpu.VMEM((32, cap, 128), BF16),
            pltpu.VMEM((depth, width), F32),
            pltpu.VMEM((depth, 2 * half), BF16),
            pltpu.VMEM((depth, half), BF16),
            pltpu.VMEM((depth, half), BF16),
            pltpu.VMEM((8, 48, half), BF16),
            pltpu.VMEM((8, 48, half), BF16),
            pltpu.VMEM((48, half), F32),
            pltpu.VMEM((48, half), F32),
            dma((32,)), dma((32,)), dma((32,)), dma((32,)),
            dma, dma, dma((8,)), dma((8,)), dma((8,)), dma((8,)), dma, dma,
        ],
        compiler_params=pltpu.CompilerParams(
            collective_id=1, has_side_effects=True, vmem_limit_bytes=56 << 20
        ),
    )(features, tokpos, counts, rows, head)


def body(
    tokens, widen_weight, narrow_weight, head_weight, predictor_rows, target_index, destination
):
    owners = lax.axis_size("tgt") * lax.axis_size("fsdp")
    devices = owners * lax.axis_size("dp")
    normed = norm_rows(tokens.astype(F32)).astype(BF16)
    hidden = jax.nn.gelu(
        jnp.dot(
            normed,
            lax.all_gather(widen_weight, "fsdp", axis=1, tiled=True),
            preferred_element_type=F32,
        ),
        approximate=False,
    ).astype(BF16)
    branch = jnp.dot(
        hidden,
        lax.all_gather(narrow_weight, "fsdp", axis=1, tiled=True),
        preferred_element_type=F32,
    )
    features = norm_rows(tokens.astype(F32) + branch).astype(BF16)
    head = lax.all_gather(head_weight, "fsdp", axis=1, tiled=True)
    cap = predictor_rows.shape[0] // owners
    routed = destination[:, 0]
    entry = jnp.arange(routed.shape[0], dtype=jnp.int32)
    earlier = (routed[:, None] == routed[None, :]) & (entry[:, None] < entry[None, :])
    position = routed * cap + jnp.sum(earlier.astype(jnp.int32), axis=0)
    token = jnp.arange(tokens.shape[0], dtype=jnp.int32)
    chosen = target_index[:, None] == token[None, :]
    tokpos = jnp.sum(jnp.where(chosen, position[:, None] + 1, 0), axis=0)[None, :] - 1
    lane = jnp.arange(128, dtype=jnp.int32)
    counts = jnp.sum((routed[:, None] == lane[None, :]).astype(jnp.int32), axis=0)[None, :]
    factor = 1.0 / math.sqrt(target_index.shape[0] * devices)
    error, grad = route(
        features, tokpos, counts, predictor_rows, head, factor,
        predictor_rows.shape[1] // lax.axis_size("fsdp"),
    )
    return (features, error, grad)


def solution(mesh):
    in_specs = (
        P(("tgt", "fsdp", "dp"), None),
        P(None, "fsdp"),
        P(None, "fsdp"),
        P(None, "fsdp"),
        P(("tgt", "fsdp", "dp"), None),
        P(("tgt", "fsdp", "dp")),
        P(("tgt", "fsdp", "dp"), None),
    )
    out_specs = (P(("tgt", "fsdp", "dp"), None), P(("tgt", "fsdp", "dp"), None), P("fsdp", None))
    return jax.shard_map(body, mesh=mesh, in_specs=in_specs, out_specs=out_specs, check_vma=False)
```

time: 504 us -> 357 us (0.71)
  waiting for transfers between devices: 396 us -> 191 us
  Pallas kernels: 0 us -> 91.7 us
  starting transfers between devices: 16.4 us -> 0.11 us
  other arithmetic: 16 us -> 8.49 us
  matrix products: 50.4 us -> 43.6 us
    unnamed x6 -> x3, waiting for transfers between devices: 118 us -> 2.06 us
    pallas_call x0 -> x1, Pallas kernels: none -> 91.7 us  [route(): pl.pallas_call(functools.partial(route_kernel, factor, cap), out_shape=(j...]
    psum x1 -> x0, waiting for transfers between devices: 84 us -> none  [body(): gathered_total = lax.psum(shared, ('tgt', 'dp')).astype(jnp.float32)]
    all_gather x1, waiting for transfers between devices: 46.4 us -> 29.1 us  [body(): head = lax.all_gather(head_weight, 'fsdp', axis=1, tiled=True)]
    all_to_all x2 -> x0, starting transfers between devices: 16.2 us -> none  [the longest x1 9.43 us: body(): lax.all_to_all(counts.reshape(owners, 1), ('tgt', 'fsdp'), split_axis=0,...]
    all_gather x1, waiting for transfers between devices: 80.8 us -> 93.4 us  [body(): lax.all_gather(widen_weight, 'fsdp', axis=1, tiled=True)]
    dot_general x2 -> x0, matrix products: 6.62 us -> none  [the longest x1 3.91 us: body(): jnp.dot(predictor_rows, lax.all_gather(head_weight, 'fsdp', axis=1, tiled...]
    scatter x1 -> x0, other arithmetic: 6.25 us -> none  [body(): jnp.zeros((owners * capacity, width_model), jnp.bfloat16).at[position]]
  transfers between devices with their start and end apart: 7 -> 3, of which waited for: 5 -> 3; matrix products, arithmetic and copies ran while one was open for 12% -> 11% of each run, Pallas kernels for 0% -> 0%
where the time goes in v1:
time: 357 us; the launch traced here: 356 us
  waiting for transfers between devices  191 us (54%)
  Pallas kernels  91.7 us (26%)
  matrix products  43.6 us (12%)
  between operations  13.8 us (4%)
  other arithmetic  8.49 us (2%)
  local copies, waits for them, and re-layouts  8.09 us (2%)
    all_gather x1, waiting for transfers between devices, body(): lax.all_gather(widen_weight, 'fsdp', axis=1, tiled=True)  93.4 us
    pallas_call x1, Pallas kernels, route(): pl.pallas_call(functools.partial(route_kernel, factor, cap), out_shape=(j...  91.7 us
    all_gather x1, waiting for transfers between devices, body(): lax.all_gather(narrow_weight, 'fsdp', axis=1, tiled=True)  66.1 us
    dot_general x1, matrix products, body(): jnp.dot(normed, lax.all_gather(widen_weight, 'fsdp', axis=1, tiled=True),...  30.6 us
    all_gather x1, waiting for transfers between devices, body(): head = lax.all_gather(head_weight, 'fsdp', axis=1, tiled=True)  29.1 us
    dot_general x1, matrix products, body(): jnp.dot(hidden, lax.all_gather(narrow_weight, 'fsdp', axis=1, tiled=True)...  13 us
  transfers between devices with their start and end apart: 3, of which 3 were waited for; matrix products, arithmetic and copies ran while one was open for 11% of the time, Pallas kernels for 0%

profile of v1, /device:TPU:1, one launch (start us, length us, event | category | flops | bytes accessed | tf_op | source)
XLA Modules:
  0.0 356.5 jit_solution(11939380539913777062)
XLA Ops:
  7.2 0.0 all-gather.8.cloned.1.call-start
  7.2 0.7 all-gather.8.cloned.1.call-update
  7.9 0.0 all-gather.4.cloned.1.call-start
  7.9 0.7 all-gather.4.cloned.1.call-update
  8.6 0.0 all-gather.6.cloned.1.call-start
  8.7 0.7 all-gather.6.cloned.1.call-update
  9.4 0.9 convert_reduce_fusion.1
  10.3 0.7 add_add_fusion
  10.9 0.8 select_reduce_fusion
  11.8 0.6 sub.27.tokpos
  12.3 1.3 convert_reduce_fusion.2
  13.7 1.5 convert_reduce_fusion
  15.1 1.7 fusion.16
  16.8 29.1 %all-gather.8.cloned.1.call-done = bf16[384,1408]{0,1:T(8,128)(2,1)} async-done(((bf16[384,88]{0,1:T(8,128)(2,1)}), bf16[384,1408]{0,1:T(8,128)(2,1)}) %all-gather.8.cloned.1.call-update) | async-done | bytes 1081360 | tf_op jit(solution)/shard_map/all_gather | solution.py:291
  45.9 2.3 copy.12.head
  48.3 93.4 %all-gather.4.cloned.1.call-done = bf16[1408,6144]{1,0:T(8,128)(2,1)} async-done(((bf16[1408,384]{1,0:T(8,128)(2,1)}), bf16[1408,6144]{1,0:T(8,128)(2,1)}) %all-gather.4.cloned.1.call-update) | async-done | bytes 17301520 | tf_op jit(solution)/shard_map/all_gather | solution.py:280
  141.7 30.6 %fusion.13.clone.4 = bf16[384,6144]{1,0:T(8,128)(2,1)} fusion(bf16[1408,6144]{1,0:T(8,128)(2,1)} %all-gather.4.cloned.1.call-done, bf16[384,1408]{1,0:T(8,128)(2,1)} %param.7, f32[384]{0:T(512)S(1)} %add_rsqrt_fusion.1, f32[384]{0:T(512)S(1)} %broadcast_multiply_fusion.1), kind=kOutput, calls=%fused_computation.3.clone.clone.clone.clone.clone.clone.1 | convolution fusion | flops 6799294464 | bytes 23104512 | tf_op jit(solution)/shard_map/dot_general | solution.py:278
  172.3 66.1 %all-gather.6.cloned.1.call-done = bf16[6144,1408]{0,1:T(8,128)(2,1)} async-done(((bf16[6144,88]{0,1:T(8,128)(2,1)}), bf16[6144,1408]{0,1:T(8,128)(2,1)}) %all-gather.6.cloned.1.call-update) | async-done | bytes 17301520 | tf_op jit(solution)/shard_map/all_gather | solution.py:287
  238.4 13.0 %fusion.53 = (f32[384]{0:T(512)S(1)}, f32[384,1408]{1,0:T(8,128)S(1)}) fusion(bf16[6144,1408]{0,1:T(8,128)(2,1)} %all-gather.6.cloned.1.call-done, bf16[384,1408]{1,0:T(8,128)(2,1)S(1)} %copy-done, bf16[384,6144]{1,0:T(8,128)(2,1)} %fusion.13.clone.4), kind=kOutput, calls=%fused_computation.75 | convolution fusion | flops 6645399040 | bytes 25265664 | tf_op jit(solution)/shard_map/dot_general | solution.py:285
  251.4 0.4 multiply_reduce_fusion
  251.8 1.3 multiply_convert_fusion.feat
  253.1 91.7 %shard_map.94 = (bf16[1024,1408]{1,0:T(8,128)(2,1)}, f32[24,1408]{1,0:T(8,128)}) custom-call(bf16[384,1408]{1,0:T(8,128)(2,1)} %multiply_convert_fusion.feat, s32[1,384]{1,0:T(1,128)} %sub.27.tokpos, s32[1,128]{1,0:T(1,128)} %bitcast.19, bf16[1024,384]{1,0:T(8,128)(2,1)} %rows.1, bf16[384,1408]{1,0:T(8,128)(2,1)} %copy.12.head), custom_call_target="tpu_custom_call" | custom-call | tf_op jit(solution)/shard_map/pallas_call | solution.py:240
  344.8 3.6 %copy.15 = bf16[1024,1408]{1,0:T(8,128)(2,1)} copy(bf16[1024,1408]{1,0:T(8,128)(2,1)} %get-tuple-element.13) | data formatting | bytes 5767168
  348.4 1.6 copy.16
  (7 shorter events, 0.0 us)
Async XLA Ops:
  7.2 38.8 %all-gather.8.cloned.1.call-start = ((), (), s32[]{:S(2)}) async-start(), calls=%async_computation.2 | async-start | bytes 1148928 | tf_op jit(solution)/shard_map/all_gather | solution.py:291
  7.9 133.8 %all-gather.4.cloned.1.call-start = ((), (), s32[]{:S(2)}) async-start(), calls=%async_computation | async-start | bytes 18382848 | tf_op jit(solution)/shard_map/all_gather | solution.py:280
  8.6 229.7 %all-gather.6.cloned.1.call-start = ((), (), s32[]{:S(2)}) async-start(), calls=%async_computation.1 | async-start | bytes 18382848 | tf_op jit(solution)/shard_map/all_gather | solution.py:287
  48.3 190.1 %copy-start = (bf16[384,1408]{1,0:T(8,128)(2,1)S(1)}, bf16[384,1408]{1,0:T(8,128)(2,1)}, u32[]{:S(2)}) copy-start(bf16[384,1408]{1,0:T(8,128)(2,1)} %param.7) | copy-start | bytes 3244036
Sparse Core Ops, SparseCore 0:
  9.7 36.1 all-gather.7
  47.6 94.0 all-gather.3
  143.4 94.9 all-gather.5

commit v2 on v1

--- a/solution.py
+++ b/solution.py
@@ -39,6 +39,285 @@
 
 def wait_send(src, sem, target):
     pltpu.make_async_remote_copy(src, src, sem, sem, device_id=target, device_id_type=MESH).wait_send()
+
+
+def gelu(v):
+    return 0.5 * v * (1.0 + lax.erf(v * math.sqrt(0.5)))
+
+
+def encode_kernel(
+    tokens, widen, narrow_t, head_t, feats, head_out,
+    xs, w1, w2, hid, nar, nar_in, heads, kept, pp_out, pp_in, pc_out, pc_in, py_out, py_in, summed,
+    s_xp, r_xp, s_xy, r_xy, s_xf, r_xf, s_wp, r_wp, s_wx, r_wx, s_wz, r_wz,
+    s_np, r_np, s_nx, r_nx, s_nz, r_nz, s_hx, r_hx, s_hz, r_hz, s_hp, r_hp,
+    s_pp, r_pp, s_pc, r_pc, s_py, r_py,
+):
+    x, y, z, c = place()
+    zl, p = lax.rem(z, 2), lax.rem(y, 2)
+    partner = device(x, y, z, 1 - c)
+    y_up, y_down = lax.rem(y + 1, 4), lax.rem(y + 3, 4)
+    z_up = device(x, y, lax.rem(z + 1, 4), c)
+    z_down = device(x, y, lax.rem(z + 3, 4), c)
+    ahead = lax.select(c == 0, y_up, y_down)
+    behind = lax.select(c == 0, y_down, y_up)
+    helper, helped = device(x, ahead, z, c), device(x, behind, z, c)
+    steps, back = (0, 1, 3, 2), (0, 2, 1, 3)
+
+    def at_x(step):
+        return lax.rem(x + step, 4)
+
+    def across(step):
+        return device(at_x(step), y, z, c)
+
+    ring = c == zl
+
+    barrier = pltpu.get_barrier_semaphore()
+    for other in (partner, helper, helped, z_up, z_down, across(1), across(2), across(3)):
+        pl.semaphore_signal(barrier, inc=1, device_id=other, device_id_type=MESH)
+
+    xs[0] = norm_rows(tokens[...].astype(F32)).astype(BF16)
+    for group in range(2):
+        for k in range(4):
+            unit = (8 * group + 2 * k + p) * 384
+            nar[group, :88, 384 * k : 384 * (k + 1)] = narrow_t[:, pl.ds(pl.multiple_of(unit, 384), 384)]
+    nar[:, 88:, :] = jnp.zeros((2, 8, 1536), BF16)
+    heads[zl, x, c, :88, :] = head_t[...]
+    heads[zl, x, c, 88:, :] = jnp.zeros((8, 384), BF16)
+    w2[0, 704:, :] = jnp.zeros((64, 1536), BF16)
+    w2[1, :64, :] = jnp.zeros((64, 1536), BF16)
+    pl.semaphore_wait(barrier, 8)
+
+    def spread_z(at):
+        send(w1.at[at, pl.ds(0, 704)], w1.at[at, pl.ds(0, 704)], s_wz.at[at, 0], r_wz.at[at, 0], z_up)
+        send(w1.at[at, pl.ds(704, 704)], w1.at[at, pl.ds(704, 704)], s_wz.at[at, 1], r_wz.at[at, 1], z_down)
+
+    def spread_x():
+        for k in (1, 2, 3):
+            send(w1.at[x], w1.at[x], s_wx.at[k], r_wx.at[back[k]], across(steps[k]))
+
+    @pl.when((c == p) & (c != zl))
+    def _():
+        send(widen, w1.at[x], s_wp, r_wp, partner)
+
+    send(xs.at[0], xs.at[2 + c], s_xy, r_xy, helper)
+
+    @pl.when((c == p) & ring)
+    def _():
+        w1[x] = widen[...]
+        spread_x()
+        spread_z(x)
+
+    send(xs.at[0], xs.at[1], s_xp, r_xp, partner)
+    send(nar.at[1 - c], nar_in, s_np, r_np, partner)
+
+    @pl.when((c != p) & ring)
+    def _():
+        wait_recv(w1.at[x], r_wp, partner)
+        spread_x()
+        spread_z(x)
+
+    def hidden(slot, at):
+        block = jnp.dot(xs[slot], w1[at], preferred_element_type=F32)
+        hid[slot, :, pl.ds(pl.multiple_of(at * 384, 384), 384)] = gelu(block).astype(BF16)
+
+    def piece(side, at):
+        return pl.multiple_of(64 * side + 176 * at, 16)
+
+    def spread_narrow_z(at):
+        row = piece(zl, at)
+        upper, lower = w2.at[zl, pl.ds(row, 96)], w2.at[zl, pl.ds(row + 96, 80)]
+        send(upper, upper, s_nz.at[at, 0], r_nz.at[at, 0], z_up)
+        send(lower, lower, s_nz.at[at, 1], r_nz.at[at, 1], z_down)
+
+    def spread_head_z(at):
+        src = heads.at[zl, at, c]
+
+        @pl.when(lax.rem(at, 2) == 0)
+        def _():
+            send(src, src, s_hz.at[at], r_hz.at[at], z_up)
+
+        @pl.when(lax.rem(at, 2) == 1)
+        def _():
+            send(src, src, s_hz.at[at], r_hz.at[at], z_down)
+
+    def arrive_widen(k):
+        at = at_x(steps[k])
+        if k:
+            @pl.when(ring)
+            def _():
+                wait_recv(w1.at[at], r_wx.at[k], partner)
+                spread_z(at)
+
+        @pl.when(jnp.logical_not(ring))
+        def _():
+            wait_recv(w1.at[at, pl.ds(0, 704)], r_wz.at[at, 0], partner)
+            wait_recv(w1.at[at, pl.ds(704, 704)], r_wz.at[at, 1], partner)
+
+        return at
+
+    wait_recv(nar_in, r_np, partner)
+    mine, other = nar[c, :88, :].astype(F32), nar_in[:88, :].astype(F32)
+    row = piece(zl, x)
+
+    @pl.when(c == 0)
+    def _():
+        w2[zl, pl.ds(row, 176), :] = jnp.concatenate([mine, other], axis=0).astype(BF16)
+
+    @pl.when(c == 1)
+    def _():
+        w2[zl, pl.ds(row, 176), :] = jnp.concatenate([other, mine], axis=0).astype(BF16)
+
+    spread_narrow_z(x)
+    at = arrive_widen(0)
+    hidden(0, at)
+    wait_recv(xs.at[1], r_xp, partner)
+    hidden(1, at)
+    own = w2.at[zl, pl.ds(row, 176)]
+    for k in (1, 2, 3):
+        send(own, own, s_nx.at[k], r_nx.at[back[k]], across(steps[k]))
+    own_head = heads.at[zl, x, c]
+    for k in (1, 2, 3):
+        send(own_head, own_head, s_hx.at[k], r_hx.at[back[k]], across(steps[k]))
+    wait_recv(xs.at[2 + c], r_xy, partner)
+    send(xs.at[2 + c], xs.at[2 + c], s_xf, r_xf, partner)
+    hidden(2 + c, at)
+    wait_recv(xs.at[3 - c], r_xf, partner)
+    hidden(3 - c, at)
+    spread_head_z(x)
+
+    for k in (1, 2, 3):
+        at = arrive_widen(k)
+
+        def fill(slot, _):
+            hidden(slot, at)
+            return 0
+
+        lax.fori_loop(0, 4, fill, 0)
+
+    for k in (1, 2, 3):
+        at = at_x(steps[k])
+        wait_recv(w2.at[zl, pl.ds(piece(zl, at), 176)], r_nx.at[k], partner)
+        spread_narrow_z(at)
+    for k in (1, 2, 3):
+        at = at_x(steps[k])
+        wait_recv(heads.at[zl, at, c], r_hx.at[k], partner)
+        spread_head_z(at)
+
+    def partial(slot, side):
+        return lax.dot_general(
+            hid[slot], w2[side], (((1,), (1,)), ((), ())), preferred_element_type=F32
+        )
+
+    def add(value, side):
+        @pl.when(side == 0)
+        def _():
+            summed[:, :768] += value
+
+        @pl.when(side == 1)
+        def _():
+            summed[:, 640:] += value
+
+    summed[...] = tokens[...].astype(F32)
+    for turn in range(2):
+        side = zl if turn == 0 else 1 - zl
+        if turn == 1:
+            for k in range(4):
+                row = piece(side, at_x(steps[k]))
+                at = at_x(steps[k])
+                wait_recv(w2.at[side, pl.ds(row, 96)], r_nz.at[at, 0], partner)
+                wait_recv(w2.at[side, pl.ds(row + 96, 80)], r_nz.at[at, 1], partner)
+        pc_out[turn] = partial(3 - c, side).astype(BF16)
+        send(pc_out.at[turn], pc_in.at[turn], s_pc.at[turn], r_pc.at[turn], partner)
+        kept[...] = partial(2 + c, side)
+        wait_recv(pc_in.at[turn], r_pc.at[turn], partner)
+        py_out[turn] = (kept[...] + pc_in[turn].astype(F32)).astype(BF16)
+        send(py_out.at[turn], py_in.at[turn], s_py.at[turn], r_py.at[turn], helped)
+        pp_out[turn] = partial(1, side).astype(BF16)
+        send(pp_out.at[turn], pp_in.at[turn], s_pp.at[turn], r_pp.at[turn], partner)
+        add(partial(0, side), side)
+
+    for k in range(4):
+        at = at_x(steps[k])
+        wait_recv(heads.at[1 - zl, at, c], r_hz.at[at], partner)
+    send(heads.at[:, :, c], heads.at[:, :, c], s_hp, r_hp, partner)
+    for turn in range(2):
+        side = zl if turn == 0 else 1 - zl
+        wait_recv(pp_in.at[turn], r_pp.at[turn], partner)
+        add(pp_in[turn].astype(F32), side)
+        if turn == 1:
+            wait_recv(heads.at[:, :, 1 - c], r_hp, partner)
+            for k in range(8):
+                both = [heads[k // 4, k % 4, core, :88, :].astype(F32) for core in range(2)]
+                head_out[k] = jnp.concatenate(both, axis=0).astype(BF16)
+        wait_recv(py_in.at[turn], r_py.at[turn], partner)
+        add(py_in[turn].astype(F32), side)
+    feats[...] = norm_rows(summed[...]).astype(BF16)
+
+    @pl.when((c == p) & (c != zl))
+    def _():
+        wait_send(widen, s_wp, partner)
+
+    wait_send(xs.at[0], s_xy, partner)
+    wait_send(xs.at[0], s_xp, partner)
+    wait_send(xs.at[2 + c], s_xf, partner)
+    wait_send(nar.at[1 - c], s_np, partner)
+    wait_send(heads.at[:, :, c], s_hp, partner)
+    for k in range(4):
+        at = at_x(steps[k])
+        row = piece(zl, at)
+
+        @pl.when(ring)
+        def _():
+            if k:
+                wait_send(w1.at[x], s_wx.at[k], partner)
+            wait_send(w1.at[at, pl.ds(0, 704)], s_wz.at[at, 0], partner)
+            wait_send(w1.at[at, pl.ds(704, 704)], s_wz.at[at, 1], partner)
+
+        if k:
+            wait_send(own, s_nx.at[k], partner)
+            wait_send(own_head, s_hx.at[k], partner)
+        wait_send(w2.at[zl, pl.ds(row, 96)], s_nz.at[at, 0], partner)
+        wait_send(w2.at[zl, pl.ds(row + 96, 80)], s_nz.at[at, 1], partner)
+        wait_send(heads.at[zl, at, c], s_hz.at[at], partner)
+    for turn in range(2):
+        wait_send(pc_out.at[turn], s_pc.at[turn], partner)
+        wait_send(py_out.at[turn], s_py.at[turn], partner)
+        wait_send(pp_out.at[turn], s_pp.at[turn], partner)
+
+
+def encode(tokens, widen_weight, narrow_weight, head_weight):
+    rows, width = tokens.shape
+    dma = pltpu.SemaphoreType.DMA
+    vmem = pl.BlockSpec(memory_space=pltpu.VMEM)
+    part = pltpu.VMEM((2, rows, 768), BF16)
+    return pl.pallas_call(
+        encode_kernel,
+        out_shape=(
+            jax.ShapeDtypeStruct((rows, width), BF16),
+            jax.ShapeDtypeStruct((8, 176, 384), BF16),
+        ),
+        in_specs=[vmem] * 4,
+        out_specs=(vmem, vmem),
+        scratch_shapes=[
+            pltpu.VMEM((4, rows, width), BF16),
+            pltpu.VMEM((4, width, 384), BF16),
+            pltpu.VMEM((2, 768, 1536), BF16),
+            pltpu.VMEM((4, rows, 1536), BF16),
+            pltpu.VMEM((2, 96, 1536), BF16),
+            pltpu.VMEM((96, 1536), BF16),
+            pltpu.VMEM((2, 4, 2, 96, 384), BF16),
+            pltpu.VMEM((rows, 768), F32),
+            part, part, part, part, part, part,
+            pltpu.VMEM((rows, width), F32),
+            dma, dma, dma, dma, dma, dma, dma, dma, dma((4,)), dma((4,)), dma((4, 2)), dma((4, 2)),
+            dma, dma, dma((4,)), dma((4,)), dma((4, 2)), dma((4, 2)),
+            dma((4,)), dma((4,)), dma((4,)), dma((4,)), dma, dma,
+            dma((2,)), dma((2,)), dma((2,)), dma((2,)), dma((2,)), dma((2,)),
+        ],
+        compiler_params=pltpu.CompilerParams(
+            collective_id=2, has_side_effects=True, vmem_limit_bytes=56 << 20
+        ),
+    )(tokens, widen_weight, narrow_weight.T, head_weight.T)
 
 
 def route_kernel(
@@ -115,7 +394,9 @@
 
     def predict(i, _):
         rows_at = pl.ds(pl.multiple_of(i * 128, 128), 128)
-        pred[rows_at, :] = jnp.dot(rows[rows_at, :], head[...], preferred_element_type=F32)
+        pred[rows_at, :] = lax.dot_general(
+            rows[rows_at, :], head[...], (((1,), (1,)), ((), ())), preferred_element_type=F32
+        )
         return 0
 
     lax.fori_loop(0, owners * cap // 128, predict, 0)
@@ -273,22 +554,8 @@
 ):
     owners = lax.axis_size("tgt") * lax.axis_size("fsdp")
     devices = owners * lax.axis_size("dp")
-    normed = norm_rows(tokens.astype(F32)).astype(BF16)
-    hidden = jax.nn.gelu(
-        jnp.dot(
-            normed,
-            lax.all_gather(widen_weight, "fsdp", axis=1, tiled=True),
-            preferred_element_type=F32,
-        ),
-        approximate=False,
-    ).astype(BF16)
-    branch = jnp.dot(
-        hidden,
-        lax.all_gather(narrow_weight, "fsdp", axis=1, tiled=True),
-        preferred_element_type=F32,
-    )
-    features = norm_rows(tokens.astype(F32) + branch).astype(BF16)
-    head = lax.all_gather(head_weight, "fsdp", axis=1, tiled=True)
+    features, head = encode(tokens, widen_weight, narrow_weight, head_weight)
+    head = head.reshape(features.shape[1], predictor_rows.shape[1])
     cap = predictor_rows.shape[0] // owners
     routed = destination[:, 0]
     entry = jnp.arange(routed.shape[0], dtype=jnp.int32)

time: 357 us -> 194 us (0.54)
  waiting for transfers between devices: 191 us -> 0 us
  Pallas kernels: 91.7 us -> 183 us
  matrix products: 43.6 us -> 0 us
  between operations: 13.8 us -> 0.67 us
  other arithmetic: 8.49 us -> 3.69 us
    all_gather x3 -> x0, waiting for transfers between devices: 189 us -> none  [the longest x1 93.4 us: body(): lax.all_gather(widen_weight, 'fsdp', axis=1, tiled=True)]
    pallas_call x0 -> x1, Pallas kernels: none -> 95.4 us  [encode(): pl.pallas_call(encode_kernel, out_shape=(jax.ShapeDtypeStruct((rows, widt...]
    dot_general x2 -> x0, matrix products: 43.6 us -> none  [the longest x1 30.6 us: body(): jnp.dot(normed, lax.all_gather(widen_weight, 'fsdp', axis=1, tiled=True),...]
    pallas_call x1, Pallas kernels: 91.7 us -> 87.9 us  [route(): pl.pallas_call(functools.partial(route_kernel, factor, cap), out_shape=(j...]
  transfers between devices with their start and end apart: 3 -> 0, of which waited for: 3 -> 0; matrix products, arithmetic and copies ran while one was open for 11% -> 0% of each run, Pallas kernels for 0% -> 0%
where the time goes in v2:
time: 194 us
  Pallas kernels  183 us (94%)
  local copies, waits for them, and re-layouts  5.86 us (3%)
  other arithmetic  3.69 us (2%)
    pallas_call x1, Pallas kernels, encode(): pl.pallas_call(encode_kernel, out_shape=(jax.ShapeDtypeStruct((rows, widt...  95.4 us
    pallas_call x1, Pallas kernels, route(): pl.pallas_call(functools.partial(route_kernel, factor, cap), out_shape=(j...  87.9 us
    unnamed x7, local copies, waits for them, and re-layouts  5.29 us

profile of v2, /device:TPU:1, one launch (start us, length us, event | category | flops | bytes accessed | tf_op | source)
XLA Modules:
  0.0 193.6 jit_solution(13036467803111666413)
XLA Ops:
  0.6 1.3 convert_reduce_fusion.1
  1.9 0.9 convert_reduce_fusion
  2.8 0.7 add_add_fusion
  3.5 0.8 select_reduce_fusion
  4.3 0.6 sub.7.tokpos
  4.9 95.4 %shard_map.94 = (bf16[384,1408]{1,0:T(8,128)(2,1)}, bf16[8,176,384]{2,1,0:T(8,128)(2,1)}) custom-call(bf16[384,1408]{1,0:T(8,128)(2,1)} %tokens.1, bf16[1408,384]{1,0:T(8,128)(2,1)} %widen.1, bf16[88,6144]{1,0:T(8,128)(2,1)} %bitcast.8, bf16[88,384]{1,0:T(8,128)(2,1)} %bitcast.9), custom_call_target="tpu_custom_call" | custom-call | tf_op jit(solution)/shard_map/pallas_call | solution.py:293
  100.4 0.0 copy-start
  100.4 87.9 %shard_map.95 = (bf16[1024,1408]{1,0:T(8,128)(2,1)}, f32[24,1408]{1,0:T(8,128)}) custom-call(bf16[384,1408]{1,0:T(8,128)(2,1)} %get-tuple-element.14.feat, s32[1,384]{1,0:T(1,128)} %sub.7.tokpos, s32[1,128]{1,0:T(1,128)} %bitcast.14, bf16[1024,384]{1,0:T(8,128)(2,1)} %rows.1, bf16[1408,384]{1,0:T(8,128)(2,1)} %bitcast.7), custom_call_target="tpu_custom_call" | custom-call | tf_op jit(solution)/shard_map/pallas_call | solution.py:521
  188.3 0.0 copy-done
  188.3 1.0 copy.13
  189.3 0.0 copy-start.1
  189.3 3.6 %copy.14 = bf16[1024,1408]{1,0:T(8,128)(2,1)} copy(bf16[1024,1408]{1,0:T(8,128)(2,1)} %get-tuple-element.15) | data formatting | bytes 5767168
  192.9 0.0 copy-done.1
  192.9 0.7 copy.15
  (1 shorter events, 0.0 us)
Async XLA Ops:
  100.4 87.9 %copy-start = (bf16[384,1408]{1,0:T(8,128)(2,1)S(1)}, bf16[384,1408]{1,0:T(8,128)(2,1)}, u32[]{:S(2)}) copy-start(bf16[384,1408]{1,0:T(8,128)(2,1)} %get-tuple-element.14.feat) | copy-start | bytes 3244036
  189.3 3.6 %copy-start.1 = (f32[24,1408]{1,0:T(8,128)S(1)}, f32[24,1408]{1,0:T(8,128)}, u32[]{:S(2)}) copy-start(f32[24,1408]{1,0:T(8,128)} %get-tuple-element.16) | copy-start | bytes 405508

commit v3 on v2

--- a/solution.py
+++ b/solution.py
@@ -50,7 +50,7 @@
     xs, w1, w2, hid, nar, nar_in, heads, kept, pp_out, pp_in, pc_out, pc_in, py_out, py_in, summed,
     s_xp, r_xp, s_xy, r_xy, s_xf, r_xf, s_wp, r_wp, s_wx, r_wx, s_wz, r_wz,
     s_np, r_np, s_nx, r_nx, s_nz, r_nz, s_hx, r_hx, s_hz, r_hz, s_hp, r_hp,
-    s_pp, r_pp, s_pc, r_pc, s_py, r_py,
+    s_pp, r_pp, s_pc, r_pc, s_py, r_py, s_wf, r_wf, s_nf, r_nf,
 ):
     x, y, z, c = place()
     zl, p = lax.rem(z, 2), lax.rem(y, 2)
@@ -92,13 +92,18 @@
         send(w1.at[at, pl.ds(704, 704)], w1.at[at, pl.ds(704, 704)], s_wz.at[at, 1], r_wz.at[at, 1], z_down)
 
     def spread_x():
-        for k in (1, 2, 3):
+        for k in (1, 2):
             send(w1.at[x], w1.at[x], s_wx.at[k], r_wx.at[back[k]], across(steps[k]))
 
+    def pass_x(at, k):
+        half = w1.at[at, pl.ds(0, 704)] if k == 2 else w1.at[at, pl.ds(704, 704)]
+        send(half, half, s_wf.at[k], r_wf.at[k], across(4 - steps[k]))
+
     @pl.when((c == p) & (c != zl))
     def _():
         send(widen, w1.at[x], s_wp, r_wp, partner)
 
+    send(nar.at[1 - c], nar_in, s_np, r_np, partner)
     send(xs.at[0], xs.at[2 + c], s_xy, r_xy, helper)
 
     @pl.when((c == p) & ring)
@@ -108,7 +113,6 @@
         spread_z(x)
 
     send(xs.at[0], xs.at[1], s_xp, r_xp, partner)
-    send(nar.at[1 - c], nar_in, s_np, r_np, partner)
 
     @pl.when((c != p) & ring)
     def _():
@@ -120,84 +124,132 @@
         block = jnp.dot(xs[slot], w1[at], preferred_element_type=F32)
         hid[slot, :, pl.ds(pl.multiple_of(at * 384, 384), 384)] = gelu(block).astype(BF16)
 
-    def piece(side, at):
-        return pl.multiple_of(64 * side + 176 * at, 16)
-
-    def spread_narrow_z(at):
-        row = piece(zl, at)
-        upper, lower = w2.at[zl, pl.ds(row, 96)], w2.at[zl, pl.ds(row + 96, 80)]
-        send(upper, upper, s_nz.at[at, 0], r_nz.at[at, 0], z_up)
-        send(lower, lower, s_nz.at[at, 1], r_nz.at[at, 1], z_down)
-
-    def spread_head_z(at):
-        src = heads.at[zl, at, c]
-
-        @pl.when(lax.rem(at, 2) == 0)
-        def _():
-            send(src, src, s_hz.at[at], r_hz.at[at], z_up)
-
-        @pl.when(lax.rem(at, 2) == 1)
-        def _():
-            send(src, src, s_hz.at[at], r_hz.at[at], z_down)
-
-    def arrive_widen(k):
-        at = at_x(steps[k])
-        if k:
-            @pl.when(ring)
-            def _():
-                wait_recv(w1.at[at], r_wx.at[k], partner)
-                spread_z(at)
-
-        @pl.when(jnp.logical_not(ring))
-        def _():
-            wait_recv(w1.at[at, pl.ds(0, 704)], r_wz.at[at, 0], partner)
-            wait_recv(w1.at[at, pl.ds(704, 704)], r_wz.at[at, 1], partner)
-
-        return at
-
-    wait_recv(nar_in, r_np, partner)
-    mine, other = nar[c, :88, :].astype(F32), nar_in[:88, :].astype(F32)
-    row = piece(zl, x)
-
-    @pl.when(c == 0)
-    def _():
-        w2[zl, pl.ds(row, 176), :] = jnp.concatenate([mine, other], axis=0).astype(BF16)
-
-    @pl.when(c == 1)
-    def _():
-        w2[zl, pl.ds(row, 176), :] = jnp.concatenate([other, mine], axis=0).astype(BF16)
-
-    spread_narrow_z(x)
-    at = arrive_widen(0)
-    hidden(0, at)
-    wait_recv(xs.at[1], r_xp, partner)
-    hidden(1, at)
-    own = w2.at[zl, pl.ds(row, 176)]
-    for k in (1, 2, 3):
-        send(own, own, s_nx.at[k], r_nx.at[back[k]], across(steps[k]))
-    own_head = heads.at[zl, x, c]
-    for k in (1, 2, 3):
-        send(own_head, own_head, s_hx.at[k], r_hx.at[back[k]], across(steps[k]))
-    wait_recv(xs.at[2 + c], r_xy, partner)
-    send(xs.at[2 + c], xs.at[2 + c], s_xf, r_xf, partner)
-    hidden(2 + c, at)
-    wait_recv(xs.at[3 - c], r_xf, partner)
-    hidden(3 - c, at)
-    spread_head_z(x)
-
-    for k in (1, 2, 3):
-        at = arrive_widen(k)
-
+    def all_hidden(at):
         def fill(slot, _):
             hidden(slot, at)
             return 0
 
         lax.fori_loop(0, 4, fill, 0)
 
-    for k in (1, 2, 3):
-        at = at_x(steps[k])
-        wait_recv(w2.at[zl, pl.ds(piece(zl, at), 176)], r_nx.at[k], partner)
+    def piece(side, at):
+        return pl.multiple_of(64 * side + 176 * at, 16)
+
+    def upper(side, at):
+        return w2.at[side, pl.ds(piece(side, at), 96)]
+
+    def lower(side, at):
+        return w2.at[side, pl.ds(pl.multiple_of(piece(side, at) + 96, 16), 80)]
+
+    def spread_narrow_z(at):
+        send(upper(zl, at), upper(zl, at), s_nz.at[at, 0], r_nz.at[at, 0], z_up)
+        send(lower(zl, at), lower(zl, at), s_nz.at[at, 1], r_nz.at[at, 1], z_down)
+
+    own = w2.at[zl, pl.ds(piece(zl, x), 176)]
+    own_head = heads.at[zl, x, c]
+
+    def spread_narrow_x():
+        for k in (1, 2):
+            send(own, own, s_nx.at[k], r_nx.at[back[k]], across(steps[k]))
+
+    def spread_head_x():
+        for k in (1, 2, 3):
+            send(own_head, own_head, s_hx.at[k], r_hx.at[back[k]], across(steps[k]))
+
+    def spread_head_z(at):
+        src = heads.at[zl, at, c]
+
+        @pl.when(lax.rem(at, 2) == 0)
+        def _():
+            send(src, src, s_hz.at[at], r_hz.at[at], z_up)
+
+        @pl.when(lax.rem(at, 2) == 1)
+        def _():
+            send(src, src, s_hz.at[at], r_hz.at[at], z_down)
+
+    def widen_near():
+        for k in (1, 2):
+            at = at_x(steps[k])
+            wait_recv(w1.at[at], r_wx.at[k], partner)
+            pass_x(at, k)
+            spread_z(at)
+
+    def widen_far():
+        at = at_x(2)
+        wait_recv(w1.at[at, pl.ds(0, 704)], r_wf.at[2], partner)
+        wait_recv(w1.at[at, pl.ds(704, 704)], r_wf.at[1], partner)
+        spread_z(at)
+
+    def widen_z(at):
+        wait_recv(w1.at[at, pl.ds(0, 704)], r_wz.at[at, 0], partner)
+        wait_recv(w1.at[at, pl.ds(704, 704)], r_wz.at[at, 1], partner)
+
+    def narrow_near():
+        for k in (1, 2):
+            at = at_x(steps[k])
+            wait_recv(w2.at[zl, pl.ds(piece(zl, at), 176)], r_nx.at[k], partner)
+            half = (upper if k == 2 else lower)(zl, at)
+            send(half, half, s_nf.at[k], r_nf.at[k], across(4 - steps[k]))
+            spread_narrow_z(at)
+
+    def narrow_far():
+        at = at_x(2)
+        wait_recv(upper(zl, at), r_nf.at[2], partner)
+        wait_recv(lower(zl, at), r_nf.at[1], partner)
         spread_narrow_z(at)
+
+    def neighbour_rows(at):
+        wait_recv(xs.at[2 + c], r_xy, partner)
+        send(xs.at[2 + c], xs.at[2 + c], s_xf, r_xf, partner)
+        hidden(2 + c, at)
+        wait_recv(xs.at[3 - c], r_xf, partner)
+        hidden(3 - c, at)
+
+    wait_recv(nar_in, r_np, partner)
+    mine, other = nar[c, :88, :].astype(F32), nar_in[:88, :].astype(F32)
+
+    @pl.when(c == 0)
+    def _():
+        own[...] = jnp.concatenate([mine, other], axis=0).astype(BF16)
+
+    @pl.when(c == 1)
+    def _():
+        own[...] = jnp.concatenate([other, mine], axis=0).astype(BF16)
+
+    spread_narrow_z(x)
+
+    @pl.when(ring)
+    def _():
+        hidden(0, x)
+        wait_recv(xs.at[1], r_xp, partner)
+        hidden(1, x)
+        widen_near()
+        spread_narrow_x()
+        spread_head_x()
+        spread_head_z(x)
+        neighbour_rows(x)
+        all_hidden(at_x(1))
+        widen_far()
+        all_hidden(at_x(3))
+        narrow_near()
+        all_hidden(at_x(2))
+        narrow_far()
+
+    @pl.when(jnp.logical_not(ring))
+    def _():
+        spread_narrow_x()
+        widen_z(x)
+        hidden(0, x)
+        wait_recv(xs.at[1], r_xp, partner)
+        hidden(1, x)
+        narrow_near()
+        spread_head_x()
+        spread_head_z(x)
+        neighbour_rows(x)
+        narrow_far()
+        for k in (1, 2, 3):
+            widen_z(at_x(steps[k]))
+            all_hidden(at_x(steps[k]))
+
     for k in (1, 2, 3):
         at = at_x(steps[k])
         wait_recv(heads.at[zl, at, c], r_hx.at[k], partner)
@@ -222,10 +274,9 @@
         side = zl if turn == 0 else 1 - zl
         if turn == 1:
             for k in range(4):
-                row = piece(side, at_x(steps[k]))
                 at = at_x(steps[k])
-                wait_recv(w2.at[side, pl.ds(row, 96)], r_nz.at[at, 0], partner)
-                wait_recv(w2.at[side, pl.ds(row + 96, 80)], r_nz.at[at, 1], partner)
+                wait_recv(upper(side, at), r_nz.at[at, 0], partner)
+                wait_recv(lower(side, at), r_nz.at[at, 1], partner)
         pc_out[turn] = partial(3 - c, side).astype(BF16)
         send(pc_out.at[turn], pc_in.at[turn], s_pc.at[turn], r_pc.at[turn], partner)
         kept[...] = partial(2 + c, side)
@@ -264,20 +315,22 @@
     wait_send(heads.at[:, :, c], s_hp, partner)
     for k in range(4):
         at = at_x(steps[k])
-        row = piece(zl, at)
 
         @pl.when(ring)
         def _():
-            if k:
+            if k in (1, 2):
                 wait_send(w1.at[x], s_wx.at[k], partner)
+                wait_send(w1.at[x, pl.ds(0, 704)], s_wf.at[k], partner)
             wait_send(w1.at[at, pl.ds(0, 704)], s_wz.at[at, 0], partner)
             wait_send(w1.at[at, pl.ds(704, 704)], s_wz.at[at, 1], partner)
 
+        if k in (1, 2):
+            wait_send(own, s_nx.at[k], partner)
+            wait_send((upper if k == 2 else lower)(zl, x), s_nf.at[k], partner)
         if k:
-            wait_send(own, s_nx.at[k], partner)
             wait_send(own_head, s_hx.at[k], partner)
-        wait_send(w2.at[zl, pl.ds(row, 96)], s_nz.at[at, 0], partner)
-        wait_send(w2.at[zl, pl.ds(row + 96, 80)], s_nz.at[at, 1], partner)
+        wait_send(upper(zl, at), s_nz.at[at, 0], partner)
+        wait_send(lower(zl, at), s_nz.at[at, 1], partner)
         wait_send(heads.at[zl, at, c], s_hz.at[at], partner)
     for turn in range(2):
         wait_send(pc_out.at[turn], s_pc.at[turn], partner)
@@ -313,6 +366,7 @@
             dma, dma, dma((4,)), dma((4,)), dma((4, 2)), dma((4, 2)),
             dma((4,)), dma((4,)), dma((4,)), dma((4,)), dma, dma,
             dma((2,)), dma((2,)), dma((2,)), dma((2,)), dma((2,)), dma((2,)),
+            dma((4,)), dma((4,)), dma((4,)), dma((4,)),
         ],
         compiler_params=pltpu.CompilerParams(
             collective_id=2, has_side_effects=True, vmem_limit_bytes=56 << 20
@@ -322,8 +376,8 @@
 
 def route_kernel(
     factor, cap, feat, tokpos, counts, rows, head, error, grad,
-    buf, rcv, pred, flags, flags_in, gsum, gpad, pair_in, shares, r1, r2, fin, fin_in,
-    s_a, r_a, s_f, r_f, s_0, r_0, s_1, r_1, s_2, r_2, s_3, r_3,
+    buf, mid_x, mid_z, rcv, pred, flags, flags_in, gsum, gpad, pair_in, shares, r1, r2, fin, fin_in,
+    s_x, r_x, s_z, r_z, s_xz, r_xz, s_zx, r_zx, s_f, r_f, s_0, r_0, s_1, r_1, s_2, r_2, s_3, r_3,
 ):
     x, y, z, c = place()
     t, zl = z // 2, lax.rem(z, 2)
@@ -366,30 +420,41 @@
 
     lax.fori_loop(1, 8, greet_group, 0)
 
-    slot_row = lax.broadcasted_iota(jnp.int32, (cap, 128), 0)
-    flags[...] = jnp.where(slot_row < counts[...], 1.0, 0.0).astype(BF16)
+    flags[...] = jnp.broadcast_to(counts[...], (16, 128)).astype(F32).astype(BF16)
 
     def fill(i, _):
-        rows_at = pl.ds(pl.multiple_of(i * 128, 128), 128)
         slot = lax.broadcasted_iota(jnp.int32, (128, feat.shape[0]), 0) + i * 128
         pick = jnp.where(slot == tokpos[...], 1.0, 0.0).astype(BF16)
-        buf[rows_at, :] = jnp.dot(pick, feat[...], preferred_element_type=F32).astype(BF16)
+        block = jnp.dot(pick, feat[...], preferred_element_type=F32).astype(BF16)
+        buf[i // 2, pl.ds(2 * lax.rem(i, 2), 2)] = block.reshape(2, 2, 2, 16, -1)
         return 0
 
     lax.fori_loop(0, owners * cap // 128, fill, 0)
 
     pl.semaphore_wait(barrier, owners - 1 + 6)
+
+    def along_x(step, core=0):
+        nx = lax.rem(x + step, 4)
+        return device(nx, y, z, lax.rem(c + core, 2)), nx
+
+    def along_z(step, core=0):
+        nz = lax.rem(z + step, 4)
+        return device(x, y, nz, lax.rem(c + core, 2)), nz
+
+    for step in (1, 3, 2):
+        target, nx = along_x(step)
+        send(buf.at[:, nx, :, 0], mid_x.at[x], s_x.at[step], r_x.at[step], target)
+        target, nz = along_z(step)
+        send(buf.at[nz, :, :, 1], mid_z.at[z], s_z.at[step], r_z.at[step], target)
+    mid_x[x] = buf[:, x, :, 0]
+    mid_z[z] = buf[z, :, :, 1]
 
     def out(r, _):
         target, o = plane(r)
         send(flags, flags_in.at[me], s_f.at[o], r_f.at[me], target)
-        src = buf.at[pl.ds(pl.multiple_of(o * cap, cap), cap)]
-        send(src, rcv.at[pl.ds(pl.multiple_of(me * cap, cap), cap)], s_a.at[o], r_a.at[me], target)
         return 0
 
     lax.fori_loop(1, owners, out, 0)
-    mine = pl.ds(pl.multiple_of(me * cap, cap), cap)
-    rcv[mine, :] = buf[mine, :]
     flags_in[me] = flags[...]
 
     def predict(i, _):
@@ -402,27 +467,45 @@
     lax.fori_loop(0, owners * cap // 128, predict, 0)
     gsum[...] = jnp.zeros_like(gsum)
 
+    for step in (1, 3, 2):
+        wait_recv(mid_x.at[lax.rem(x + 4 - step, 4)], r_x.at[step], partner)
+        wait_recv(mid_z.at[lax.rem(z + 4 - step, 4)], r_z.at[step], partner)
+    hops = [(step, core) for core in (0, 1) for step in (1, 3, 2, 0) if step + core]
+    for step, core in hops:
+        nc = lax.rem(c + core, 2)
+        at = 2 * step + core
+        target, nz = along_z(step, core)
+        send(mid_x.at[:, nz, nc], rcv.at[z, :, c, 0], s_xz.at[at], r_xz.at[at], target)
+        target, nx = along_x(step, core)
+        send(mid_z.at[:, nx, nc], rcv.at[:, x, c, 1], s_zx.at[at], r_zx.at[at], target)
+    rcv[z, :, c, 0] = mid_x[:, z, c]
+    rcv[:, x, c, 1] = mid_z[:, x, c]
+
+    def flags_from(s, _):
+        @pl.when(s != me)
+        def _():
+            wait_recv(flags_in.at[s], r_f.at[s], partner)
+
+        return 0
+
+    lax.fori_loop(0, owners, flags_from, 0)
+    for step, core in hops:
+        nc = lax.rem(c + core, 2)
+        at = 2 * step + core
+        wait_recv(rcv.at[lax.rem(z + 4 - step, 4), :, nc, 0], r_xz.at[at], partner)
+        wait_recv(rcv.at[:, lax.rem(x + 4 - step, 4), nc, 1], r_zx.at[at], partner)
+
     per = 8
 
-    def arrive(k, _):
-        i = lax.rem(z + k, 4)
-
-        def one(q, _):
-            s = i * per + q
-
-            @pl.when(s != me)
-            def _():
-                wait_recv(flags_in.at[s], r_f.at[s], partner)
-                wait_recv(rcv.at[pl.ds(pl.multiple_of(s * cap, cap), cap)], r_a.at[s], partner)
-
-            return 0
-
-        lax.fori_loop(0, per, one, 0)
+    def arrive(i, _):
         rows_at = pl.ds(pl.multiple_of(i * (per * cap), per * cap), per * cap)
-        lane = lax.broadcasted_iota(jnp.int32, (per * cap, 128), 1)
-        live = flags_in[pl.ds(i * per, per)].astype(F32).reshape(per * cap, 128)
-        live = jnp.sum(jnp.where(lane == me, live, 0.0), axis=1, keepdims=True)
-        wrong = jnp.where(live > 0.5, pred[rows_at, :] - rcv[rows_at, :].astype(F32), 0.0).astype(BF16)
+        lane = lax.broadcasted_iota(jnp.int32, (per, 16, 128), 2)
+        live = flags_in[pl.ds(i * per, per)].astype(F32)
+        live = jnp.sum(jnp.where(lane == me, live, 0.0), axis=2, keepdims=True)
+        live = jnp.broadcast_to(live[:, None], (per, 2, 16, 1)).reshape(per * cap, 1)
+        slot = lax.rem(lax.broadcasted_iota(jnp.int32, (per * cap, 1), 0), cap).astype(F32)
+        got = rcv[i].astype(F32).reshape(per * cap, -1)
+        wrong = jnp.where(slot < live, pred[rows_at, :] - got, 0.0).astype(BF16)
         error[rows_at, :] = wrong
         gsum[...] += lax.dot_general(
             rows[rows_at, :], wrong, (((0,), (0,)), ((), ())), preferred_element_type=F32
@@ -493,12 +576,17 @@
         grad[:, half:] = fin[24:, : wide - half]
 
     def done(r, _):
-        o = plane(r)[1]
-        wait_send(flags, s_f.at[o], partner)
-        wait_send(buf.at[pl.ds(pl.multiple_of(o * cap, cap), cap)], s_a.at[o], partner)
+        wait_send(flags, s_f.at[plane(r)[1]], partner)
         return 0
 
     lax.fori_loop(1, owners, done, 0)
+    for step in (1, 2, 3):
+        wait_send(mid_x.at[x], s_x.at[step], partner)
+        wait_send(mid_z.at[z], s_z.at[step], partner)
+    for step, core in hops:
+        at = 2 * step + core
+        wait_send(rcv.at[z, :, c, 0], s_xz.at[at], partner)
+        wait_send(rcv.at[:, x, c, 1], s_zx.at[at], partner)
 
     def done_shares(j, _):
         target, b = chip(j)
@@ -527,11 +615,13 @@
         in_specs=[vmem] * 5,
         out_specs=(vmem, vmem),
         scratch_shapes=[
-            pltpu.VMEM((slots, width), BF16),
-            pltpu.VMEM((slots, width), BF16),
+            pltpu.VMEM((4, 4, 2, 2, 16, width), BF16),
+            pltpu.VMEM((4, 4, 2, 16, width), BF16),
+            pltpu.VMEM((4, 4, 2, 16, width), BF16),
+            pltpu.VMEM((4, 4, 2, 2, 16, width), BF16),
             pltpu.VMEM((slots, width), F32),
-            pltpu.VMEM((cap, 128), BF16),
-            pltpu.VMEM((32, cap, 128), BF16),
+            pltpu.VMEM((16, 128), BF16),
+            pltpu.VMEM((32, 16, 128), BF16),
             pltpu.VMEM((depth, width), F32),
             pltpu.VMEM((depth, 2 * half), BF16),
             pltpu.VMEM((depth, half), BF16),
@@ -540,7 +630,8 @@
             pltpu.VMEM((8, 48, half), BF16),
             pltpu.VMEM((48, half), F32),
             pltpu.VMEM((48, half), F32),
-            dma((32,)), dma((32,)), dma((32,)), dma((32,)),
+            dma((4,)), dma((4,)), dma((4,)), dma((4,)), dma((8,)), dma((8,)), dma((8,)), dma((8,)),
+            dma((32,)), dma((32,)),
             dma, dma, dma((8,)), dma((8,)), dma((8,)), dma((8,)), dma, dma,
         ],
         compiler_params=pltpu.CompilerParams(

time: 194 us -> 167 us (0.86)
  Pallas kernels: 183 us -> 156 us
    pallas_call x1, Pallas kernels: 95.4 us -> 80.7 us  [encode(): pl.pallas_call(encode_kernel, out_shape=(jax.ShapeDtypeStruct((rows, widt...]
    pallas_call x1, Pallas kernels: 87.9 us -> 75.4 us  [route(): pl.pallas_call(functools.partial(route_kernel, factor, cap), out_shape=(j...]
where the time goes in v3:
time: 167 us; the launch traced here: 166 us
  Pallas kernels  156 us (93%)
  local copies, waits for them, and re-layouts  5.86 us (4%)
  other arithmetic  3.69 us (2%)
    pallas_call x1, Pallas kernels, encode(): pl.pallas_call(encode_kernel, out_shape=(jax.ShapeDtypeStruct((rows, widt...  80.7 us
    pallas_call x1, Pallas kernels, route(): pl.pallas_call(functools.partial(route_kernel, factor, cap), out_shape=(j...  75.4 us
    unnamed x7, local copies, waits for them, and re-layouts  5.29 us

profile of v3, /device:TPU:1, one launch (start us, length us, event | category | flops | bytes accessed | tf_op | source)
XLA Modules:
  0.0 166.3 jit_solution(10809738009722720442)
XLA Ops:
  0.6 1.3 convert_reduce_fusion.1
  1.9 0.9 convert_reduce_fusion
  2.8 0.7 add_add_fusion
  3.5 0.8 select_reduce_fusion
  4.3 0.6 sub.7.tokpos
  4.9 80.7 %shard_map.94 = (bf16[384,1408]{1,0:T(8,128)(2,1)}, bf16[8,176,384]{2,1,0:T(8,128)(2,1)}) custom-call(bf16[384,1408]{1,0:T(8,128)(2,1)} %tokens.1, bf16[1408,384]{1,0:T(8,128)(2,1)} %widen.1, bf16[88,6144]{1,0:T(8,128)(2,1)} %bitcast.8, bf16[88,384]{1,0:T(8,128)(2,1)} %bitcast.9), custom_call_target="tpu_custom_call" | custom-call | tf_op jit(solution)/shard_map/pallas_call | solution.py:346
  85.6 0.0 copy-start
  85.6 75.4 %shard_map.95 = (bf16[1024,1408]{1,0:T(8,128)(2,1)}, f32[24,1408]{1,0:T(8,128)}) custom-call(bf16[384,1408]{1,0:T(8,128)(2,1)} %get-tuple-element.14.feat, s32[1,384]{1,0:T(1,128)} %sub.7.tokpos, s32[1,128]{1,0:T(1,128)} %bitcast.14, bf16[1024,384]{1,0:T(8,128)(2,1)} %rows.1, bf16[1408,384]{1,0:T(8,128)(2,1)} %bitcast.7), custom_call_target="tpu_custom_call" | custom-call | tf_op jit(solution)/shard_map/pallas_call | solution.py:609
  161.0 0.0 copy-done
  161.0 1.0 copy.13
  162.0 0.0 copy-start.1
  162.0 3.6 %copy.14 = bf16[1024,1408]{1,0:T(8,128)(2,1)} copy(bf16[1024,1408]{1,0:T(8,128)(2,1)} %get-tuple-element.15) | data formatting | bytes 5767168
  165.6 0.0 copy-done.1
  165.6 0.7 copy.15
  (1 shorter events, 0.0 us)
Async XLA Ops:
  85.6 75.4 %copy-start = (bf16[384,1408]{1,0:T(8,128)(2,1)S(1)}, bf16[384,1408]{1,0:T(8,128)(2,1)}, u32[]{:S(2)}) copy-start(bf16[384,1408]{1,0:T(8,128)(2,1)} %get-tuple-element.14.feat) | copy-start | bytes 3244036
  162.0 3.6 %copy-start.1 = (f32[24,1408]{1,0:T(8,128)S(1)}, f32[24,1408]{1,0:T(8,128)}, u32[]{:S(2)}) copy-start(f32[24,1408]{1,0:T(8,128)} %get-tuple-element.16) | copy-start | bytes 405508

commit v4 on v3

v4 whole, which is shorter than its diff:
```python
import functools
import math

import jax
import jax.numpy as jnp
from jax import lax
from jax.experimental import pallas as pl
from jax.experimental.pallas import tpu as pltpu
from jax.sharding import PartitionSpec as P

MESH = pl.DeviceIdType.MESH
F32, BF16 = jnp.float32, jnp.bfloat16


def norm_rows(values):
    center = jnp.mean(values, axis=-1, keepdims=True)
    shifted = values - center
    spread = jnp.mean(shifted * shifted, axis=-1, keepdims=True)
    return shifted * lax.rsqrt(spread + 1e-06)


def place():
    t, f, d = lax.axis_index("tgt"), lax.axis_index("fsdp"), lax.axis_index("dp")
    return lax.rem(f // 2, 4), d, 2 * t + f // 8, lax.rem(f, 2)


def device(x, y, z, c):
    return (z // 2, lax.rem(z, 2) * 8 + x * 2 + c, y)


def send(src, dst, send_sem, recv_sem, target):
    copy = pltpu.make_async_remote_copy(src, dst, send_sem, recv_sem, device_id=target, device_id_type=MESH)
    copy.start()


def wait_recv(dst, sem, target):
    pltpu.make_async_remote_copy(dst, dst, sem, sem, device_id=target, device_id_type=MESH).wait_recv()


def wait_send(src, sem, target):
    pltpu.make_async_remote_copy(src, src, sem, sem, device_id=target, device_id_type=MESH).wait_send()


def gelu(v):
    return 0.5 * v * (1.0 + lax.erf(v * math.sqrt(0.5)))


def kernel(
    factor, cap, tokens, widen, narrow_t, head_t, rows, owner_of, token_of, feats_out, error_out, grad,
    feats, error, xs, w1, w2, hid, nar, nar_in, heads, head, kept, pp_out, pp_in, pc_out, pc_in, py_out, py_in, summed,
    buf_x, buf_z, mid_x, mid_z, rcv, pred, slot_of, flags, flags_in, gpad, pair_in, shares, r1, r2, fin, fin_in,
    s_xp, r_xp, s_xy, r_xy, s_xf, r_xf, s_wp, r_wp, s_wx, r_wx, s_wz, r_wz,
    s_np, r_np, s_nx, r_nx, s_nz, r_nz, s_hx, r_hx, s_hz, r_hz, s_hp, r_hp,
    s_pp, r_pp, s_pc, r_pc, s_py, r_py, s_wf, r_wf, s_nf, r_nf, s_mx, r_mx, s_mf, r_mf,
    s_x, r_x, s_z, r_z, s_xz, r_xz, s_zx, r_zx, s_f, r_f, s_fz, r_fz, s_o, s_0, r_0, s_1, r_1, s_2, r_2, s_3, r_3,
):
    x, y, z, c = place()
    zl, p = lax.rem(z, 2), lax.rem(y, 2)
    partner = device(x, y, z, 1 - c)
    y_up, y_down = lax.rem(y + 1, 4), lax.rem(y + 3, 4)
    z_up = device(x, y, lax.rem(z + 1, 4), c)
    z_down = device(x, y, lax.rem(z + 3, 4), c)
    ahead = lax.select(c == 0, y_up, y_down)
    behind = lax.select(c == 0, y_down, y_up)
    helper, helped = device(x, ahead, z, c), device(x, behind, z, c)
    steps, back = (0, 1, 3, 2), (0, 2, 1, 3)

    def at_x(step):
        return lax.rem(x + step, 4)

    def across(step):
        return device(at_x(step), y, z, c)

    ring = c == zl

    t = z // 2
    me = 8 * z + 2 * x + c
    owners = 32

    def along_x(step, core=0):
        nx = lax.rem(x + step, 4)
        return device(nx, y, z, lax.rem(c + core, 2)), nx

    def along_z(step, core=0):
        nz = lax.rem(z + step, 4)
        return device(x, y, nz, lax.rem(c + core, 2)), nz

    def copy_of(j):
        nt, nd = lax.rem(t + j // 4, 2), lax.rem(y + lax.rem(j, 4), 4)
        return device(x, nd, 2 * nt + zl, c), nt * 4 + nd

    def chip(j):
        nz, nx = lax.rem(zl + j // 4, 2), lax.rem(x + lax.rem(j, 4), 4)
        return device(nx, y, 2 * t + nz, c), 4 * nz + nx


    hops = [(step, core) for core in (0, 1) for step in (1, 3, 2, 0) if step + core]
    barrier = pltpu.get_barrier_semaphore()

    others = [partner]
    others += [along(step, core)[0] for along in (along_x, along_z) for core in (0, 1) for step in (1, 2, 3)]
    others += [chip(j)[0] for j in (5, 6, 7)] + [copy_of(j)[0] for j in (1, 2, 3, 5, 6, 7)]
    for other in others:
        pl.semaphore_signal(barrier, inc=1, device_id=other, device_id_type=MESH)

    xs[0] = norm_rows(tokens[...].astype(F32)).astype(BF16)
    for core in range(2):
        for k in range(4):
            unit = (8 * core + 2 * k + p) * 384
            nar[core, :88, 384 * k : 384 * (k + 1)] = narrow_t[:, pl.ds(pl.multiple_of(unit, 384), 384)]
    nar[:, 88:, :] = jnp.zeros((2, 8, 1536), BF16)
    heads[zl, x, c, :88, :] = head_t[...]
    heads[zl, x, c, 88:, :] = jnp.zeros((8, 384), BF16)
    w2[0, 704:, :] = jnp.zeros((64, 1536), BF16)
    w2[1, :64, :] = jnp.zeros((64, 1536), BF16)
    pl.semaphore_wait(barrier, len(others))

    def spread_z(at):
        send(w1.at[at, pl.ds(0, 704)], w1.at[at, pl.ds(0, 704)], s_wz.at[at, 0], r_wz.at[at, 0], z_up)
        send(w1.at[at, pl.ds(704, 704)], w1.at[at, pl.ds(704, 704)], s_wz.at[at, 1], r_wz.at[at, 1], z_down)

    def spread_x():
        for k in (1, 2):
            send(w1.at[x], w1.at[x], s_wx.at[k], r_wx.at[back[k]], across(steps[k]))

    def pass_x(at, k):
        half = w1.at[at, pl.ds(0, 704)] if k == 2 else w1.at[at, pl.ds(704, 704)]
        send(half, half, s_wf.at[k], r_wf.at[k], across(4 - steps[k]))

    @pl.when((c == p) & (c != zl))
    def _():
        send(widen, w1.at[x], s_wp, r_wp, partner)

    send(nar.at[1 - c], nar_in, s_np, r_np, partner)
    send(xs.at[0], xs.at[2 + c], s_xy, r_xy, helper)

    @pl.when((c == p) & ring)
    def _():
        w1[x] = widen[...]
        spread_x()
        spread_z(x)

    send(xs.at[0], xs.at[1], s_xp, r_xp, partner)

    @pl.when((c != p) & ring)
    def _():
        wait_recv(w1.at[x], r_wp, partner)
        spread_x()
        spread_z(x)

    def hidden(slot, at):
        block = jnp.dot(xs[slot], w1[at], preferred_element_type=F32)
        hid[slot, :, pl.ds(pl.multiple_of(at * 384, 384), 384)] = gelu(block).astype(BF16)

    def all_hidden(at):
        def fill(slot, _):
            hidden(slot, at)
            return 0

        lax.fori_loop(0, 4, fill, 0)

    def piece(side, at):
        return pl.multiple_of(64 * side + 176 * at, 16)

    def upper(side, at):
        return w2.at[side, pl.ds(piece(side, at), 96)]

    def lower(side, at):
        return w2.at[side, pl.ds(pl.multiple_of(piece(side, at) + 96, 16), 80)]

    def part(side, at, first, count):
        return w2.at[side, pl.ds(pl.multiple_of(piece(side, at) + first, 16), count)]

    def spread_narrow_z(at, top, bottom):
        up, down = part(zl, at, 0, top), part(zl, at, 176 - bottom, bottom)
        send(up, up, s_nz.at[at, 0], r_nz.at[at, 0], z_up)
        send(down, down, s_nz.at[at, 1], r_nz.at[at, 1], z_down)

    def narrow_z(at, top, bottom):
        wait_recv(part(1 - zl, at, 0, top), r_nz.at[at, 0], partner)
        wait_recv(part(1 - zl, at, 176 - bottom, bottom), r_nz.at[at, 1], partner)

    def middle_out():
        narrow_z(x, 96, 80)
        rows_mid = part(1 - zl, x, 64, 64)
        for k in (1, 2):
            send(rows_mid, rows_mid, s_mx.at[k], r_mx.at[back[k]], across(steps[k]))

    def middle_pass():
        for k in (1, 2):
            at = at_x(steps[k])
            wait_recv(part(1 - zl, at, 64, 64), r_mx.at[k], partner)
            half = part(1 - zl, at, 64 if k == 2 else 96, 32)
            send(half, half, s_mf.at[k], r_mf.at[k], across(4 - steps[k]))

    def middle_far():
        wait_recv(part(1 - zl, at_x(2), 64, 32), r_mf.at[2], partner)
        wait_recv(part(1 - zl, at_x(2), 96, 32), r_mf.at[1], partner)

    own_cols = w2.at[zl, pl.ds(piece(zl, x), 176)]
    own_head = heads.at[zl, x, c]

    def spread_narrow_x():
        for k in (1, 2):
            send(own_cols, own_cols, s_nx.at[k], r_nx.at[back[k]], across(steps[k]))

    def spread_head_x():
        for k in (1, 2, 3):
            send(own_head, own_head, s_hx.at[k], r_hx.at[back[k]], across(steps[k]))

    def spread_head_z(at):
        src = heads.at[zl, at, c]

        @pl.when(lax.rem(at, 2) == 0)
        def _():
            send(src, src, s_hz.at[at], r_hz.at[at], z_up)

        @pl.when(lax.rem(at, 2) == 1)
        def _():
            send(src, src, s_hz.at[at], r_hz.at[at], z_down)

    def widen_near():
        for k in (1, 2):
            at = at_x(steps[k])
            wait_recv(w1.at[at], r_wx.at[k], partner)
            pass_x(at, k)
            spread_z(at)

    def widen_far():
        at = at_x(2)
        wait_recv(w1.at[at, pl.ds(0, 704)], r_wf.at[2], partner)
        wait_recv(w1.at[at, pl.ds(704, 704)], r_wf.at[1], partner)
        spread_z(at)

    def widen_z(at):
        wait_recv(w1.at[at, pl.ds(0, 704)], r_wz.at[at, 0], partner)
        wait_recv(w1.at[at, pl.ds(704, 704)], r_wz.at[at, 1], partner)

    def narrow_near():
        for k in (1, 2):
            at = at_x(steps[k])
            wait_recv(w2.at[zl, pl.ds(piece(zl, at), 176)], r_nx.at[k], partner)
            half = (upper if k == 2 else lower)(zl, at)
            send(half, half, s_nf.at[k], r_nf.at[k], across(4 - steps[k]))
            spread_narrow_z(at, 64, 48)

    def narrow_far():
        at = at_x(2)
        wait_recv(upper(zl, at), r_nf.at[2], partner)
        wait_recv(lower(zl, at), r_nf.at[1], partner)
        spread_narrow_z(at, 64, 48)

    def indices():
        count = owner_of.shape[1]
        owner = owner_of[...]
        one = jnp.where(lax.broadcasted_iota(jnp.int32, (128, count), 0) == owner, 1.0, 0.0)
        before = lax.broadcasted_iota(jnp.int32, (count, count), 0) < lax.broadcasted_iota(
            jnp.int32, (count, count), 1
        )
        rank = jnp.dot(one.astype(BF16), jnp.where(before, 1.0, 0.0).astype(BF16), preferred_element_type=F32)
        rank = jnp.sum(rank * one, axis=0, keepdims=True)
        flags[...] = lax.dot_general(
            jnp.ones((16, count), BF16), one.astype(BF16), (((1,), (1,)), ((), ())), preferred_element_type=F32
        ).astype(BF16)
        flags_in[z, x, c] = flags[...]
        line = lax.broadcasted_iota(jnp.int32, (8, count), 0)
        known = jnp.where(line == 0, owner.astype(F32) + 1.0, rank).astype(BF16)
        here = lax.broadcasted_iota(jnp.int32, (tokens.shape[0], count), 0) == token_of[...]
        found = lax.dot_general(
            known, jnp.where(here, 1.0, 0.0).astype(BF16), (((1,), (1,)), ((), ())), preferred_element_type=F32
        )
        slot_of[...] = jnp.broadcast_to((found[0:1] - 1.0) * cap + found[1:2], slot_of.shape)

        for step, core in hops:
            at = 2 * step + core
            send(flags, flags_in.at[z, x, c], s_f.at[at], r_f.at[at], along_x(step, core)[0])

    def spread_flags():
        for step, core in hops:
            source = flags_in.at[z, lax.rem(x + 4 - step, 4), lax.rem(c + core, 2)]
            wait_recv(source, r_f.at[2 * step + core], partner)
        for step in (1, 3, 2):
            send(flags_in.at[z], flags_in.at[z], s_fz.at[step], r_fz.at[step], along_z(step)[0])

    def neighbour_rows(at):
        wait_recv(xs.at[2 + c], r_xy, partner)
        send(xs.at[2 + c], xs.at[2 + c], s_xf, r_xf, partner)
        hidden(2 + c, at)
        wait_recv(xs.at[3 - c], r_xf, partner)
        hidden(3 - c, at)

    wait_recv(nar_in, r_np, partner)
    mine, other = nar[c, :88, :].astype(F32), nar_in[:88, :].astype(F32)

    @pl.when(c == 0)
    def _():
        own_cols[...] = jnp.concatenate([mine, other], axis=0).astype(BF16)

    @pl.when(c == 1)
    def _():
        own_cols[...] = jnp.concatenate([other, mine], axis=0).astype(BF16)

    spread_narrow_z(x, 96, 80)

    @pl.when(ring)
    def _():
        hidden(0, x)
        wait_recv(xs.at[1], r_xp, partner)
        hidden(1, x)
        widen_near()
        spread_narrow_x()
        middle_out()
        indices()
        neighbour_rows(x)
        all_hidden(at_x(1))
        widen_far()
        all_hidden(at_x(3))
        narrow_near()
        middle_pass()
        all_hidden(at_x(2))
        narrow_far()

    @pl.when(jnp.logical_not(ring))
    def _():
        spread_narrow_x()
        widen_z(x)
        hidden(0, x)
        wait_recv(xs.at[1], r_xp, partner)
        hidden(1, x)
        narrow_near()
        middle_out()
        indices()
        neighbour_rows(x)
        narrow_far()
        middle_pass()
        for k in (1, 2, 3):
            widen_z(at_x(steps[k]))
            all_hidden(at_x(steps[k]))

    spread_head_x()
    spread_head_z(x)
    spread_flags()

    def partial(slot, side):
        return lax.dot_general(
            hid[slot], w2[side], (((1,), (1,)), ((), ())), preferred_element_type=F32
        )

    def add(value, side):
        @pl.when(side == 0)
        def _():
            summed[:, :768] += value

        @pl.when(side == 1)
        def _():
            summed[:, 640:] += value

    summed[...] = tokens[...].astype(F32)
    for turn in range(2):
        side = zl if turn == 0 else 1 - zl
        if turn == 1:
            middle_far()
            for k in (1, 2, 3):
                narrow_z(at_x(steps[k]), 64, 48)
        pc_out[turn] = partial(3 - c, side).astype(BF16)
        send(pc_out.at[turn], pc_in.at[turn], s_pc.at[turn], r_pc.at[turn], partner)
        kept[...] = partial(2 + c, side)
        wait_recv(pc_in.at[turn], r_pc.at[turn], partner)
        py_out[turn] = (kept[...] + pc_in[turn].astype(F32)).astype(BF16)
        send(py_out.at[turn], py_in.at[turn], s_py.at[turn], r_py.at[turn], helped)
        pp_out[turn] = partial(1, side).astype(BF16)
        send(pp_out.at[turn], pp_in.at[turn], s_pp.at[turn], r_pp.at[turn], partner)
        add(partial(0, side), side)
        if turn == 0:
            for k in (1, 2, 3):
                at = at_x(steps[k])
                wait_recv(heads.at[zl, at, c], r_hx.at[k], partner)
                spread_head_z(at)

    for k in range(4):
        at = at_x(steps[k])
        wait_recv(heads.at[1 - zl, at, c], r_hz.at[at], partner)
    send(heads.at[:, :, c], heads.at[:, :, c], s_hp, r_hp, partner)
    for turn in range(2):
        side = zl if turn == 0 else 1 - zl
        wait_recv(pp_in.at[turn], r_pp.at[turn], partner)
        add(pp_in[turn].astype(F32), side)
        wait_recv(py_in.at[turn], r_py.at[turn], partner)
        add(py_in[turn].astype(F32), side)
    feats[...] = norm_rows(summed[...]).astype(BF16)
    pltpu.make_async_copy(feats, feats_out, s_o.at[4]).start()


    line = lax.broadcasted_iota(jnp.int32, (128, feats.shape[0]), 0)
    outer, inner = line // 32, lax.rem(line // 16, 2) * cap + lax.rem(line, 16)

    def rows_for(slot):
        pick = jnp.where(slot.astype(F32) == slot_of[0:1], 1.0, 0.0).astype(BF16)
        return jnp.dot(pick, feats[...], preferred_element_type=F32).astype(BF16).reshape(4, 2, 16, -1)

    for step in (1, 3, 2):
        target, nx = along_x(step)
        buf_x[nx] = rows_for(outer * (8 * cap) + inner + nx * (2 * cap))
        send(buf_x.at[nx], mid_x.at[x], s_x.at[step], r_x.at[step], target)
        target, nz = along_z(step)
        buf_z[nz] = rows_for(outer * (2 * cap) + inner + nz * (8 * cap) + 16)
        send(buf_z.at[nz], mid_z.at[z], s_z.at[step], r_z.at[step], target)
    mid_x[x] = rows_for(outer * (8 * cap) + inner + x * (2 * cap))
    mid_z[z] = rows_for(outer * (2 * cap) + inner + z * (8 * cap) + 16)

    wait_recv(heads.at[:, :, 1 - c], r_hp, partner)
    for k in range(8):
        both = [heads[k // 4, k % 4, core, :88, :].astype(F32) for core in range(2)]
        head[k] = jnp.concatenate(both, axis=0).astype(BF16)

    def predict(i, _):
        rows_at = pl.ds(pl.multiple_of(i * 128, 128), 128)
        pred[rows_at, :] = lax.dot_general(
            rows[rows_at, :], head[...].reshape(-1, rows.shape[1]), (((1,), (1,)), ((), ())), preferred_element_type=F32
        )
        return 0

    lax.fori_loop(0, owners * cap // 128, predict, 0)
    summed[...] = jnp.zeros_like(summed)

    for step in (1, 3, 2):
        wait_recv(mid_x.at[lax.rem(x + 4 - step, 4)], r_x.at[step], partner)
        wait_recv(mid_z.at[lax.rem(z + 4 - step, 4)], r_z.at[step], partner)
    for step, core in hops:
        nc = lax.rem(c + core, 2)
        at = 2 * step + core
        target, nz = along_z(step, core)
        send(mid_x.at[:, nz, nc], rcv.at[z, :, c, 0], s_xz.at[at], r_xz.at[at], target)
        target, nx = along_x(step, core)
        send(mid_z.at[:, nx, nc], rcv.at[:, x, c, 1], s_zx.at[at], r_zx.at[at], target)
    rcv[z, :, c, 0] = mid_x[:, z, c]
    rcv[:, x, c, 1] = mid_z[:, x, c]

    for step in (1, 3, 2):
        wait_recv(flags_in.at[lax.rem(z + 4 - step, 4)], r_fz.at[step], partner)
    for step, core in hops:
        nc = lax.rem(c + core, 2)
        at = 2 * step + core
        wait_recv(rcv.at[lax.rem(z + 4 - step, 4), :, nc, 0], r_xz.at[at], partner)
        wait_recv(rcv.at[:, lax.rem(x + 4 - step, 4), nc, 1], r_zx.at[at], partner)

    per = 8

    def arrive(i, _):
        rows_at = pl.ds(pl.multiple_of(i * (per * cap), per * cap), per * cap)
        lane = lax.broadcasted_iota(jnp.int32, (per, 16, 128), 2)
        live = flags_in[i].reshape(per, 16, 128).astype(F32)
        live = jnp.sum(jnp.where(lane == me, live, 0.0), axis=2, keepdims=True)
        live = jnp.broadcast_to(live[:, None], (per, 2, 16, 1)).reshape(per * cap, 1)
        slot = lax.rem(lax.broadcasted_iota(jnp.int32, (per * cap, 1), 0), cap).astype(F32)
        got = rcv[i].astype(F32).reshape(per * cap, -1)
        wrong = jnp.where(slot < live, pred[rows_at, :] - got, 0.0).astype(BF16)
        error[rows_at, :] = wrong
        pltpu.make_async_copy(error.at[rows_at], error_out.at[rows_at], s_o.at[i]).start()
        summed[...] += lax.dot_general(
            rows[rows_at, :], wrong, (((0,), (0,)), ((), ())), preferred_element_type=F32
        )
        return 0

    lax.fori_loop(0, 4, arrive, 0)

    wide = summed.shape[1]
    half = gpad.shape[1] // 2
    gpad[:, :wide] = summed[...].astype(BF16)
    gpad[:, wide:] = jnp.zeros((gpad.shape[0], 2 * half - wide), BF16)
    theirs = pl.ds(pl.multiple_of((1 - c) * half, half), half)
    ours = pl.ds(pl.multiple_of(c * half, half), half)
    send(gpad.at[:, theirs], pair_in, s_0, r_0, partner)
    wait_recv(pair_in, r_0, partner)
    shares[...] = (gpad[:, ours].astype(F32) + pair_in[...].astype(F32)).astype(BF16)

    block = 48

    def share(j, _):
        target, b = chip(j)
        send(shares.at[pl.ds(pl.multiple_of(b * block, 16), block)], r1.at[j], s_1.at[j], r_1.at[j], target)
        return 0

    lax.fori_loop(1, 8, share, 0)
    own = shares[pl.ds(pl.multiple_of((4 * zl + x) * block, 16), block), :].astype(F32)

    def take(j, total):
        wait_recv(r1.at[j], r_1.at[j], partner)
        return total + r1[j].astype(F32)

    own = lax.fori_loop(1, 8, take, own)
    mine_at = t * 4 + y
    r2[mine_at] = own.astype(BF16)

    def spread(j, _):
        target, b = copy_of(j)
        send(r2.at[mine_at], r2.at[mine_at], s_2.at[b], r_2.at[mine_at], target)
        return 0

    lax.fori_loop(1, 8, spread, 0)

    def settle(b, _):
        @pl.when(b != mine_at)
        def _():
            wait_recv(r2.at[b], r_2.at[b], partner)

        return 0

    lax.fori_loop(0, 8, settle, 0)

    def add_copy(b, total):
        return total + r2[b].astype(F32)

    fin[...] = lax.fori_loop(0, 8, add_copy, jnp.zeros(fin.shape, F32)) * factor
    send(fin, fin_in, s_3, r_3, partner)
    wait_recv(fin_in, r_3, partner)

    @pl.when(c == 0)
    def _():
        grad[:, :half] = fin[:24, :]
        grad[:, half:] = fin_in[:24, : wide - half]

    @pl.when(c == 1)
    def _():
        grad[:, :half] = fin_in[24:, :]
        grad[:, half:] = fin[24:, : wide - half]

    for step in (1, 2, 3):
        wait_send(flags_in.at[z], s_fz.at[step], partner)
        wait_send(mid_x.at[x], s_x.at[step], partner)
        wait_send(mid_z.at[z], s_z.at[step], partner)
    for step, core in hops:
        at = 2 * step + core
        wait_send(flags, s_f.at[at], partner)
        wait_send(rcv.at[z, :, c, 0], s_xz.at[at], partner)
        wait_send(rcv.at[:, x, c, 1], s_zx.at[at], partner)

    pltpu.make_async_copy(feats, feats_out, s_o.at[4]).wait()
    for i in range(4):
        rows_at = pl.ds(i * per * cap, per * cap)
        pltpu.make_async_copy(error.at[rows_at], error_out.at[rows_at], s_o.at[i]).wait()

    def done_shares(j, _):
        target, b = chip(j)
        wait_send(shares.at[pl.ds(pl.multiple_of(b * block, 16), block)], s_1.at[j], partner)
        wait_send(r2.at[mine_at], s_2.at[copy_of(j)[1]], partner)
        return 0

    lax.fori_loop(1, 8, done_shares, 0)
    wait_send(gpad.at[:, theirs], s_0, partner)
    wait_send(fin, s_3, partner)
    @pl.when((c == p) & (c != zl))
    def _():
        wait_send(widen, s_wp, partner)

    wait_send(xs.at[0], s_xy, partner)
    wait_send(xs.at[0], s_xp, partner)
    wait_send(xs.at[2 + c], s_xf, partner)
    wait_send(nar.at[1 - c], s_np, partner)
    wait_send(heads.at[:, :, c], s_hp, partner)
    for k in range(4):
        at = at_x(steps[k])

        @pl.when(ring)
        def _():
            if k in (1, 2):
                wait_send(w1.at[x], s_wx.at[k], partner)
                wait_send(w1.at[x, pl.ds(0, 704)], s_wf.at[k], partner)
            wait_send(w1.at[at, pl.ds(0, 704)], s_wz.at[at, 0], partner)
            wait_send(w1.at[at, pl.ds(704, 704)], s_wz.at[at, 1], partner)

        if k in (1, 2):
            wait_send(own_cols, s_nx.at[k], partner)
            wait_send((upper if k == 2 else lower)(zl, x), s_nf.at[k], partner)
            wait_send(part(zl, x, 0, 64), s_mx.at[k], partner)
            wait_send(part(zl, x, 0, 32), s_mf.at[k], partner)
        if k:
            wait_send(own_head, s_hx.at[k], partner)
        wait_send(part(zl, at, 0, 64 if k else 96), s_nz.at[at, 0], partner)
        wait_send(part(zl, at, 0, 48 if k else 80), s_nz.at[at, 1], partner)
        wait_send(heads.at[zl, at, c], s_hz.at[at], partner)
    for turn in range(2):
        wait_send(pc_out.at[turn], s_pc.at[turn], partner)
        wait_send(py_out.at[turn], s_py.at[turn], partner)
        wait_send(pp_out.at[turn], s_pp.at[turn], partner)


def step(tokens, widen_weight, narrow_weight, head_weight, predictor_rows, owner_of, token_of, factor):
    count, width = tokens.shape
    slots, depth = predictor_rows.shape
    owners = lax.axis_size("tgt") * lax.axis_size("fsdp")
    cap, half = slots // owners, 768
    dma = pltpu.SemaphoreType.DMA
    vmem = pl.BlockSpec(memory_space=pltpu.VMEM)
    part = pltpu.VMEM((2, count, half), BF16)
    return pl.pallas_call(
        functools.partial(kernel, factor, cap),
        out_shape=(
            jax.ShapeDtypeStruct((count, width), BF16),
            jax.ShapeDtypeStruct((slots, width), BF16),
            jax.ShapeDtypeStruct((depth // lax.axis_size("fsdp"), width), F32),
        ),
        in_specs=[vmem] * 7,
        out_specs=(pl.BlockSpec(memory_space=pl.ANY), pl.BlockSpec(memory_space=pl.ANY), vmem),
        scratch_shapes=[
            pltpu.VMEM((count, width), BF16),
            pltpu.VMEM((slots, width), BF16),
            pltpu.VMEM((4, count, width), BF16),
            pltpu.VMEM((4, width, 384), BF16),
            pltpu.VMEM((2, 768, 1536), BF16),
            pltpu.VMEM((4, count, 1536), BF16),
            pltpu.VMEM((2, 96, 1536), BF16),
            pltpu.VMEM((96, 1536), BF16),
            pltpu.VMEM((2, 4, 2, 96, depth), BF16),
            pltpu.VMEM((8, 176, depth), BF16),
            pltpu.VMEM((count, half), F32),
            part, part, part, part, part, part,
            pltpu.VMEM((count, width), F32),
            pltpu.VMEM((4, 4, 2, 16, width), BF16),
            pltpu.VMEM((4, 4, 2, 16, width), BF16),
            pltpu.VMEM((4, 4, 2, 16, width), BF16),
            pltpu.VMEM((4, 4, 2, 16, width), BF16),
            pltpu.VMEM((4, 4, 2, 2, 16, width), BF16),
            pltpu.VMEM((slots, width), F32),
            pltpu.VMEM((8, count), F32),
            pltpu.VMEM((16, 128), BF16),
            pltpu.VMEM((4, 4, 2, 16, 128), BF16),
            pltpu.VMEM((depth, 2 * half), BF16),
            pltpu.VMEM((depth, half), BF16),
            pltpu.VMEM((depth, half), BF16),
            pltpu.VMEM((8, 48, half), BF16),
            pltpu.VMEM((8, 48, half), BF16),
            pltpu.VMEM((48, half), F32),
            pltpu.VMEM((48, half), F32),
            dma, dma, dma, dma, dma, dma, dma, dma, dma((4,)), dma((4,)), dma((4, 2)), dma((4, 2)),
            dma, dma, dma((4,)), dma((4,)), dma((4, 2)), dma((4, 2)),
            dma((4,)), dma((4,)), dma((4,)), dma((4,)), dma, dma,
            dma((2,)), dma((2,)), dma((2,)), dma((2,)), dma((2,)), dma((2,)),
            dma((4,)), dma((4,)), dma((4,)), dma((4,)), dma((4,)), dma((4,)), dma((4,)), dma((4,)),
            dma((4,)), dma((4,)), dma((4,)), dma((4,)), dma((8,)), dma((8,)), dma((8,)), dma((8,)),
            dma((8,)), dma((8,)), dma((4,)), dma((4,)), dma((5,)),
            dma, dma, dma((8,)), dma((8,)), dma((8,)), dma((8,)), dma, dma,
        ],
        compiler_params=pltpu.CompilerParams(
            collective_id=1, has_side_effects=True, vmem_limit_bytes=62 << 20
        ),
    )(
        tokens, widen_weight, narrow_weight.T, head_weight.T, predictor_rows, owner_of, token_of
    )


def body(
    tokens, widen_weight, narrow_weight, head_weight, predictor_rows, target_index, destination
):
    devices = lax.axis_size("tgt") * lax.axis_size("fsdp") * lax.axis_size("dp")
    entries = target_index.shape[0]
    return step(
        tokens, widen_weight, narrow_weight, head_weight, predictor_rows,
        destination.reshape(1, entries), target_index.reshape(1, entries),
        1.0 / math.sqrt(entries * devices),
    )


def solution(mesh):
    in_specs = (
        P(("tgt", "fsdp", "dp"), None),
        P(None, "fsdp"),
        P(None, "fsdp"),
        P(None, "fsdp"),
        P(("tgt", "fsdp", "dp"), None),
        P(("tgt", "fsdp", "dp")),
        P(("tgt", "fsdp", "dp"), None),
    )
    out_specs = (P(("tgt", "fsdp", "dp"), None), P(("tgt", "fsdp", "dp"), None), P("fsdp", None))
    return jax.shard_map(body, mesh=mesh, in_specs=in_specs, out_specs=out_specs, check_vma=False)
```

time: 167 us -> 156 us (0.934)
  Pallas kernels: 156 us -> 147 us
  other arithmetic: 3.69 us -> 0 us
    pallas_call x2 -> x1, Pallas kernels: 156 us -> 147 us  [step(): pl.pallas_call(functools.partial(kernel, factor, cap), out_shape=(jax.Sha...]
    reduce_sum x3 -> x0, other arithmetic: 3 us -> none  [the longest x1 1.31 us: body(): jnp.sum((routed[:, None] == lane[None, :]).astype(jnp.int32), axis=0)]
    unnamed x7 -> x5, local copies, waits for them, and re-layouts: 5.29 us -> 6.6 us
where the time goes in v4:
time: 156 us; the launch traced here: 154 us
  Pallas kernels  147 us (94%)
  local copies, waits for them, and re-layouts  6.6 us (4%)
    pallas_call x1, Pallas kernels, step(): pl.pallas_call(functools.partial(kernel, factor, cap), out_shape=(jax.Sha...  147 us
    unnamed x5, local copies, waits for them, and re-layouts  6.6 us

profile of v4, /device:TPU:1, one launch (start us, length us, event | category | flops | bytes accessed | tf_op | source)
XLA Modules:
  0.0 153.9 jit_solution(11321178315848166626)
XLA Ops:
  0.6 146.6 %shard_map.94 = (bf16[384,1408]{1,0:T(8,128)(2,1)}, bf16[1024,1408]{1,0:T(8,128)(2,1)}, f32[24,1408]{1,0:T(8,128)}) custom-call(bf16[384,1408]{1,0:T(8,128)(2,1)} %tokens.1, bf16[1408,384]{1,0:T(8,128)(2,1)} %widen.1, bf16[88,6144]{1,0:T(8,128)(2,1)} %bitcast.4, bf16[88,384]{1,0:T(8,128)(2,1)} %bitcast.5, bf16[1024,384]{1,0:T(8,128)(2,1)} %rows.1, ...), custom_call_target="tpu_custom_call" | custom-call | tf_op jit(solution)/shard_map/pallas_call | solution.py:596
  147.3 2.3 %copy.13 = bf16[384,1408]{1,0:T(8,128)(2,1)} copy(bf16[384,1408]{1,0:T(8,128)(2,1)} %get-tuple-element.6) | data formatting | bytes 2162688
  149.6 0.0 copy-start
  149.6 3.6 %copy.14 = bf16[1024,1408]{1,0:T(8,128)(2,1)} copy(bf16[1024,1408]{1,0:T(8,128)(2,1)} %get-tuple-element.7) | data formatting | bytes 5767168
  153.2 0.0 copy-done
  153.2 0.7 copy.15
Async XLA Ops:
  149.6 3.6 %copy-start = (f32[24,1408]{1,0:T(8,128)S(1)}, f32[24,1408]{1,0:T(8,128)}, u32[]{:S(2)}) copy-start(f32[24,1408]{1,0:T(8,128)} %get-tuple-element.8) | copy-start | bytes 405508

commit v5 on v4

--- a/solution.py
+++ b/solution.py
@@ -48,7 +48,7 @@
 def kernel(
     factor, cap, tokens, widen, narrow_t, head_t, rows, owner_of, token_of, feats_out, error_out, grad,
     feats, error, xs, w1, w2, hid, nar, nar_in, heads, head, kept, pp_out, pp_in, pc_out, pc_in, py_out, py_in, summed,
-    buf_x, buf_z, mid_x, mid_z, rcv, pred, slot_of, flags, flags_in, gpad, pair_in, shares, r1, r2, fin, fin_in,
+    buf_x, buf_z, mid_x, mid_z, rcv, pred, slot_of, flags, flags_in, pair_out, pair_in, shares, r1, r_own, r2, fin, gout,
     s_xp, r_xp, s_xy, r_xy, s_xf, r_xf, s_wp, r_wp, s_wx, r_wx, s_wz, r_wz,
     s_np, r_np, s_nx, r_nx, s_nz, r_nz, s_hx, r_hx, s_hz, r_hz, s_hp, r_hp,
     s_pp, r_pp, s_pc, r_pc, s_py, r_py, s_wf, r_wf, s_nf, r_nf, s_mx, r_mx, s_mf, r_mf,
@@ -100,6 +100,7 @@
     others = [partner]
     others += [along(step, core)[0] for along in (along_x, along_z) for core in (0, 1) for step in (1, 2, 3)]
     others += [chip(j)[0] for j in (5, 6, 7)] + [copy_of(j)[0] for j in (1, 2, 3, 5, 6, 7)]
+    others += [device(x, lax.rem(y + dy, 4), lax.rem(z + dz, 4), 1 - c) for dz in (0, 2) for dy in (1, 2, 3)]
     for other in others:
         pl.semaphore_signal(barrier, inc=1, device_id=other, device_id_type=MESH)
 
@@ -121,11 +122,11 @@
 
     def spread_x():
         for k in (1, 2):
-            send(w1.at[x], w1.at[x], s_wx.at[k], r_wx.at[back[k]], across(steps[k]))
+            send(w1.at[x], w1.at[x], s_wx.at[k - 1], r_wx.at[back[k] - 1], across(steps[k]))
 
     def pass_x(at, k):
         half = w1.at[at, pl.ds(0, 704)] if k == 2 else w1.at[at, pl.ds(704, 704)]
-        send(half, half, s_wf.at[k], r_wf.at[k], across(4 - steps[k]))
+        send(half, half, s_wf.at[k - 1], r_wf.at[k - 1], across(4 - steps[k]))
 
     @pl.when((c == p) & (c != zl))
     def _():
@@ -159,6 +160,10 @@
 
         lax.fori_loop(0, 4, fill, 0)
 
+    def half_hidden(first, at):
+        hidden(first, at)
+        hidden(first + 1, at)
+
     def piece(side, at):
         return pl.multiple_of(64 * side + 176 * at, 16)
 
@@ -184,25 +189,25 @@
         narrow_z(x, 96, 80)
         rows_mid = part(1 - zl, x, 64, 64)
         for k in (1, 2):
-            send(rows_mid, rows_mid, s_mx.at[k], r_mx.at[back[k]], across(steps[k]))
+            send(rows_mid, rows_mid, s_mx.at[k - 1], r_mx.at[back[k] - 1], across(steps[k]))
 
     def middle_pass():
         for k in (1, 2):
             at = at_x(steps[k])
-            wait_recv(part(1 - zl, at, 64, 64), r_mx.at[k], partner)
+            wait_recv(part(1 - zl, at, 64, 64), r_mx.at[k - 1], partner)
             half = part(1 - zl, at, 64 if k == 2 else 96, 32)
-            send(half, half, s_mf.at[k], r_mf.at[k], across(4 - steps[k]))
+            send(half, half, s_mf.at[k - 1], r_mf.at[k - 1], across(4 - steps[k]))
 
     def middle_far():
-        wait_recv(part(1 - zl, at_x(2), 64, 32), r_mf.at[2], partner)
-        wait_recv(part(1 - zl, at_x(2), 96, 32), r_mf.at[1], partner)
+        wait_recv(part(1 - zl, at_x(2), 64, 32), r_mf.at[1], partner)
+        wait_recv(part(1 - zl, at_x(2), 96, 32), r_mf.at[0], partner)
 
     own_cols = w2.at[zl, pl.ds(piece(zl, x), 176)]
     own_head = heads.at[zl, x, c]
 
     def spread_narrow_x():
         for k in (1, 2):
-            send(own_cols, own_cols, s_nx.at[k], r_nx.at[back[k]], across(steps[k]))
+            send(own_cols, own_cols, s_nx.at[k - 1], r_nx.at[back[k] - 1], across(steps[k]))
 
     def spread_head_x():
         for k in (1, 2, 3):
@@ -222,14 +227,14 @@
     def widen_near():
         for k in (1, 2):
             at = at_x(steps[k])
-            wait_recv(w1.at[at], r_wx.at[k], partner)
+            wait_recv(w1.at[at], r_wx.at[k - 1], partner)
             pass_x(at, k)
             spread_z(at)
 
     def widen_far():
         at = at_x(2)
-        wait_recv(w1.at[at, pl.ds(0, 704)], r_wf.at[2], partner)
-        wait_recv(w1.at[at, pl.ds(704, 704)], r_wf.at[1], partner)
+        wait_recv(w1.at[at, pl.ds(0, 704)], r_wf.at[1], partner)
+        wait_recv(w1.at[at, pl.ds(704, 704)], r_wf.at[0], partner)
         spread_z(at)
 
     def widen_z(at):
@@ -239,15 +244,15 @@
     def narrow_near():
         for k in (1, 2):
             at = at_x(steps[k])
-            wait_recv(w2.at[zl, pl.ds(piece(zl, at), 176)], r_nx.at[k], partner)
+            wait_recv(w2.at[zl, pl.ds(piece(zl, at), 176)], r_nx.at[k - 1], partner)
             half = (upper if k == 2 else lower)(zl, at)
-            send(half, half, s_nf.at[k], r_nf.at[k], across(4 - steps[k]))
+            send(half, half, s_nf.at[k - 1], r_nf.at[k - 1], across(4 - steps[k]))
             spread_narrow_z(at, 64, 48)
 
     def narrow_far():
         at = at_x(2)
-        wait_recv(upper(zl, at), r_nf.at[2], partner)
-        wait_recv(lower(zl, at), r_nf.at[1], partner)
+        wait_recv(upper(zl, at), r_nf.at[1], partner)
+        wait_recv(lower(zl, at), r_nf.at[0], partner)
         spread_narrow_z(at, 64, 48)
 
     def indices():
@@ -312,13 +317,15 @@
         middle_out()
         indices()
         neighbour_rows(x)
-        all_hidden(at_x(1))
+        half_hidden(0, at_x(1))
         widen_far()
-        all_hidden(at_x(3))
+        half_hidden(2, at_x(1))
         narrow_near()
+        half_hidden(0, at_x(3))
         middle_pass()
+        half_hidden(2, at_x(3))
+        narrow_far()
         all_hidden(at_x(2))
-        narrow_far()
 
     @pl.when(jnp.logical_not(ring))
     def _():
@@ -421,7 +428,8 @@
         return 0
 
     lax.fori_loop(0, owners * cap // 128, predict, 0)
-    summed[...] = jnp.zeros_like(summed)
+    width, half = feats.shape[1], pair_in.shape[1]
+    error[:, width:] = jnp.zeros((error.shape[0], 2 * half - width), BF16)
 
     for step in (1, 3, 2):
         wait_recv(mid_x.at[lax.rem(x + 4 - step, 4)], r_x.at[step], partner)
@@ -455,24 +463,23 @@
         slot = lax.rem(lax.broadcasted_iota(jnp.int32, (per * cap, 1), 0), cap).astype(F32)
         got = rcv[i].astype(F32).reshape(per * cap, -1)
         wrong = jnp.where(slot < live, pred[rows_at, :] - got, 0.0).astype(BF16)
-        error[rows_at, :] = wrong
-        pltpu.make_async_copy(error.at[rows_at], error_out.at[rows_at], s_o.at[i]).start()
-        summed[...] += lax.dot_general(
-            rows[rows_at, :], wrong, (((0,), (0,)), ((), ())), preferred_element_type=F32
+        error[rows_at, :width] = wrong
+        pltpu.make_async_copy(error.at[rows_at, pl.ds(0, width)], error_out.at[rows_at], s_o.at[i]).start()
+        return 0
+
+    lax.fori_loop(0, 4, arrive, 0)
+
+    def product(core):
+        columns = error[:, pl.ds(pl.multiple_of(core * half, half), half)]
+        return lax.dot_general(
+            rows[...], columns, (((0,), (0,)), ((), ())), preferred_element_type=F32
         )
-        return 0
-
-    lax.fori_loop(0, 4, arrive, 0)
-
-    wide = summed.shape[1]
-    half = gpad.shape[1] // 2
-    gpad[:, :wide] = summed[...].astype(BF16)
-    gpad[:, wide:] = jnp.zeros((gpad.shape[0], 2 * half - wide), BF16)
-    theirs = pl.ds(pl.multiple_of((1 - c) * half, half), half)
-    ours = pl.ds(pl.multiple_of(c * half, half), half)
-    send(gpad.at[:, theirs], pair_in, s_0, r_0, partner)
+
+    pair_out[...] = product(1 - c).astype(BF16)
+    send(pair_out, pair_in, s_0, r_0, partner)
+    kept[...] = product(c)
     wait_recv(pair_in, r_0, partner)
-    shares[...] = (gpad[:, ours].astype(F32) + pair_in[...].astype(F32)).astype(BF16)
+    shares[...] = (kept[...] + pair_in[...].astype(F32)).astype(BF16)
 
     block = 48
 
@@ -490,40 +497,62 @@
 
     own = lax.fori_loop(1, 8, take, own)
     mine_at = t * 4 + y
-    r2[mine_at] = own.astype(BF16)
-
-    def spread(j, _):
-        target, b = copy_of(j)
-        send(r2.at[mine_at], r2.at[mine_at], s_2.at[b], r_2.at[mine_at], target)
+    r_own[...] = own.astype(BF16)
+
+    def holder(r, core):
+        return device(x, lax.rem(r, 4), 2 * (r // 4) + zl, core)
+
+    def columns_of(r):
+        return pl.ds(pl.multiple_of(r * 128, 128), 128)
+
+    def scatter(r, _):
+        @pl.when(r != mine_at)
+        def _():
+            send(r_own.at[:, columns_of(r)], r2.at[mine_at], s_2.at[r], r_2.at[mine_at], holder(r, c))
+
         return 0
 
-    lax.fori_loop(1, 8, spread, 0)
-
-    def settle(b, _):
-        @pl.when(b != mine_at)
+    lax.fori_loop(0, 6 - c, scatter, 0)
+    made = 6 * c + mine_at
+
+    @pl.when(mine_at < 6 - c)
+    def _():
+        r2[mine_at] = r_own[:, columns_of(mine_at)]
+
+        def settle(r, _):
+            @pl.when(r != mine_at)
+            def _():
+                wait_recv(r2.at[r], r_2.at[r], partner)
+
+            return 0
+
+        lax.fori_loop(0, 8, settle, 0)
+        total = r2[0].astype(F32)
+        for r in range(1, 8):
+            total = total + r2[r].astype(F32)
+        fin[...] = (total * factor).reshape(2, 24, 128)
+
+        def hand_out(q, _):
+            r, core = q // 2, lax.rem(q, 2)
+
+            @pl.when((r != mine_at) | (core != c))
+            def _():
+                send(fin.at[core], gout.at[:, columns_of(made)], s_3.at[q], r_3.at[made], holder(r, core))
+
+            return 0
+
+        lax.fori_loop(0, 16, hand_out, 0)
+        gout[:, columns_of(made)] = fin[c]
+
+    def collect(i, _):
+        @pl.when((i != made) | (mine_at >= 6 - c))
         def _():
-            wait_recv(r2.at[b], r_2.at[b], partner)
+            wait_recv(gout.at[:, columns_of(i)], r_3.at[i], partner)
 
         return 0
 
-    lax.fori_loop(0, 8, settle, 0)
-
-    def add_copy(b, total):
-        return total + r2[b].astype(F32)
-
-    fin[...] = lax.fori_loop(0, 8, add_copy, jnp.zeros(fin.shape, F32)) * factor
-    send(fin, fin_in, s_3, r_3, partner)
-    wait_recv(fin_in, r_3, partner)
-
-    @pl.when(c == 0)
-    def _():
-        grad[:, :half] = fin[:24, :]
-        grad[:, half:] = fin_in[:24, : wide - half]
-
-    @pl.when(c == 1)
-    def _():
-        grad[:, :half] = fin_in[24:, :]
-        grad[:, half:] = fin[24:, : wide - half]
+    lax.fori_loop(0, 11, collect, 0)
+    grad[...] = gout[...]
 
     for step in (1, 2, 3):
         wait_send(flags_in.at[z], s_fz.at[step], partner)
@@ -534,21 +563,39 @@
         wait_send(flags, s_f.at[at], partner)
         wait_send(rcv.at[z, :, c, 0], s_xz.at[at], partner)
         wait_send(rcv.at[:, x, c, 1], s_zx.at[at], partner)
-
     pltpu.make_async_copy(feats, feats_out, s_o.at[4]).wait()
     for i in range(4):
         rows_at = pl.ds(i * per * cap, per * cap)
-        pltpu.make_async_copy(error.at[rows_at], error_out.at[rows_at], s_o.at[i]).wait()
+        pltpu.make_async_copy(error.at[rows_at, pl.ds(0, width)], error_out.at[rows_at], s_o.at[i]).wait()
 
     def done_shares(j, _):
         target, b = chip(j)
         wait_send(shares.at[pl.ds(pl.multiple_of(b * block, 16), block)], s_1.at[j], partner)
-        wait_send(r2.at[mine_at], s_2.at[copy_of(j)[1]], partner)
         return 0
 
     lax.fori_loop(1, 8, done_shares, 0)
-    wait_send(gpad.at[:, theirs], s_0, partner)
-    wait_send(fin, s_3, partner)
+
+    def done_scatter(r, _):
+        @pl.when(r != mine_at)
+        def _():
+            wait_send(r_own.at[:, columns_of(r)], s_2.at[r], partner)
+
+        return 0
+
+    lax.fori_loop(0, 6 - c, done_scatter, 0)
+
+    @pl.when(mine_at < 6 - c)
+    def _():
+        def handed(q, _):
+            @pl.when((q // 2 != mine_at) | (lax.rem(q, 2) != c))
+            def _():
+                wait_send(fin.at[0], s_3.at[q], partner)
+
+            return 0
+
+        lax.fori_loop(0, 16, handed, 0)
+
+    wait_send(pair_out, s_0, partner)
     @pl.when((c == p) & (c != zl))
     def _():
         wait_send(widen, s_wp, partner)
@@ -564,16 +611,16 @@
         @pl.when(ring)
         def _():
             if k in (1, 2):
-                wait_send(w1.at[x], s_wx.at[k], partner)
-                wait_send(w1.at[x, pl.ds(0, 704)], s_wf.at[k], partner)
+                wait_send(w1.at[x], s_wx.at[k - 1], partner)
+                wait_send(w1.at[x, pl.ds(0, 704)], s_wf.at[k - 1], partner)
             wait_send(w1.at[at, pl.ds(0, 704)], s_wz.at[at, 0], partner)
             wait_send(w1.at[at, pl.ds(704, 704)], s_wz.at[at, 1], partner)
 
         if k in (1, 2):
-            wait_send(own_cols, s_nx.at[k], partner)
-            wait_send((upper if k == 2 else lower)(zl, x), s_nf.at[k], partner)
-            wait_send(part(zl, x, 0, 64), s_mx.at[k], partner)
-            wait_send(part(zl, x, 0, 32), s_mf.at[k], partner)
+            wait_send(own_cols, s_nx.at[k - 1], partner)
+            wait_send((upper if k == 2 else lower)(zl, x), s_nf.at[k - 1], partner)
+            wait_send(part(zl, x, 0, 64), s_mx.at[k - 1], partner)
+            wait_send(part(zl, x, 0, 32), s_mf.at[k - 1], partner)
         if k:
             wait_send(own_head, s_hx.at[k], partner)
         wait_send(part(zl, at, 0, 64 if k else 96), s_nz.at[at, 0], partner)
@@ -604,7 +651,7 @@
         out_specs=(pl.BlockSpec(memory_space=pl.ANY), pl.BlockSpec(memory_space=pl.ANY), vmem),
         scratch_shapes=[
             pltpu.VMEM((count, width), BF16),
-            pltpu.VMEM((slots, width), BF16),
+            pltpu.VMEM((slots, 2 * half), BF16),
             pltpu.VMEM((4, count, width), BF16),
             pltpu.VMEM((4, width, 384), BF16),
             pltpu.VMEM((2, 768, 1536), BF16),
@@ -625,21 +672,22 @@
             pltpu.VMEM((8, count), F32),
             pltpu.VMEM((16, 128), BF16),
             pltpu.VMEM((4, 4, 2, 16, 128), BF16),
-            pltpu.VMEM((depth, 2 * half), BF16),
+            pltpu.VMEM((depth, half), BF16),
             pltpu.VMEM((depth, half), BF16),
             pltpu.VMEM((depth, half), BF16),
             pltpu.VMEM((8, 48, half), BF16),
-            pltpu.VMEM((8, 48, half), BF16),
-            pltpu.VMEM((48, half), F32),
-            pltpu.VMEM((48, half), F32),
-            dma, dma, dma, dma, dma, dma, dma, dma, dma((4,)), dma((4,)), dma((4, 2)), dma((4, 2)),
-            dma, dma, dma((4,)), dma((4,)), dma((4, 2)), dma((4, 2)),
+            pltpu.VMEM((48, half), BF16),
+            pltpu.VMEM((8, 48, 128), BF16),
+            pltpu.VMEM((2, 24, 128), F32),
+            pltpu.VMEM((24, width), F32),
+            dma, dma, dma, dma, dma, dma, dma, dma, dma((2,)), dma((2,)), dma((4, 2)), dma((4, 2)),
+            dma, dma, dma((2,)), dma((2,)), dma((4, 2)), dma((4, 2)),
             dma((4,)), dma((4,)), dma((4,)), dma((4,)), dma, dma,
             dma((2,)), dma((2,)), dma((2,)), dma((2,)), dma((2,)), dma((2,)),
-            dma((4,)), dma((4,)), dma((4,)), dma((4,)), dma((4,)), dma((4,)), dma((4,)), dma((4,)),
+            dma((2,)), dma((2,)), dma((2,)), dma((2,)), dma((2,)), dma((2,)), dma((2,)), dma((2,)),
             dma((4,)), dma((4,)), dma((4,)), dma((4,)), dma((8,)), dma((8,)), dma((8,)), dma((8,)),
             dma((8,)), dma((8,)), dma((4,)), dma((4,)), dma((5,)),
-            dma, dma, dma((8,)), dma((8,)), dma((8,)), dma((8,)), dma, dma,
+            dma, dma, dma((8,)), dma((8,)), dma((8,)), dma((8,)), dma((16,)), dma((11,)),
         ],
         compiler_params=pltpu.CompilerParams(
             collective_id=1, has_side_effects=True, vmem_limit_bytes=62 << 20
@@ -654,11 +702,31 @@
 ):
     devices = lax.axis_size("tgt") * lax.axis_size("fsdp") * lax.axis_size("dp")
     entries = target_index.shape[0]
-    return step(
+    return move(*step(
         tokens, widen_weight, narrow_weight, head_weight, predictor_rows,
         destination.reshape(1, entries), target_index.reshape(1, entries),
         1.0 / math.sqrt(entries * devices),
-    )
+    ))
+
+
+def move_kernel(a, b, d, a_out, b_out, d_out):
+    a_out[...] = a[...]
+    b_out[...] = b[...]
+    d_out[...] = d[...]
+
+
+def move(a, b, d):
+    wide = a.shape[1]
+    first = pl.BlockSpec((a.shape[0] // 4, wide), lambda i: (i, 0))
+    second = pl.BlockSpec((b.shape[0] // 4, wide), lambda i: (i, 0))
+    third = pl.BlockSpec(d.shape, lambda i: (0, 0))
+    return pl.pallas_call(
+        move_kernel,
+        grid=(4,),
+        out_shape=tuple(jax.ShapeDtypeStruct(o.shape, o.dtype) for o in (a, b, d)),
+        in_specs=[first, second, third],
+        out_specs=(first, second, third),
+    )(a, b, d)
 
 
 def solution(mesh):

time: 156 us -> 153 us (0.981); the launches traced: 154 us -> 153 us
  local copies, waits for them, and re-layouts: 6.6 us -> 0 us
  Pallas kernels: 147 us -> 152 us
    unnamed x5 -> x0, local copies, waits for them, and re-layouts: 6.6 us -> none
    pallas_call x0 -> x1, Pallas kernels: none -> 4.66 us  [move(): pl.pallas_call(move_kernel, grid=(4,), out_shape=tuple((jax.ShapeDtypeStr...]
where the time goes in v5:
time: 153 us
  Pallas kernels  152 us (99%)
    pallas_call x1, Pallas kernels, step(): pl.pallas_call(functools.partial(kernel, factor, cap), out_shape=(jax.Sha...  147 us
    pallas_call x1, Pallas kernels, move(): pl.pallas_call(move_kernel, grid=(4,), out_shape=tuple((jax.ShapeDtypeStr...  4.66 us

profile of v5, /device:TPU:1, one launch (start us, length us, event | category | flops | bytes accessed | tf_op | source)
XLA Modules:
  0.0 152.5 jit_solution(10439273337428586312)
XLA Ops:
  0.6 147.0 %shard_map.94 = (bf16[384,1408]{1,0:T(8,128)(2,1)}, bf16[1024,1408]{1,0:T(8,128)(2,1)}, f32[24,1408]{1,0:T(8,128)}) custom-call(bf16[384,1408]{1,0:T(8,128)(2,1)} %tokens.1, bf16[1408,384]{1,0:T(8,128)(2,1)} %widen.1, bf16[88,6144]{1,0:T(8,128)(2,1)} %bitcast.4, bf16[88,384]{1,0:T(8,128)(2,1)} %bitcast.5, bf16[1024,384]{1,0:T(8,128)(2,1)} %rows.1, ...), custom_call_target="tpu_custom_call" | custom-call | tf_op jit(solution)/shard_map/pallas_call | solution.py:643
  147.7 4.7 %shard_map.95 = (bf16[384,1408]{1,0:T(8,128)(2,1)}, bf16[1024,1408]{1,0:T(8,128)(2,1)}, f32[24,1408]{1,0:T(8,128)}) custom-call(bf16[384,1408]{1,0:T(8,128)(2,1)} %get-tuple-element.6.a, bf16[1024,1408]{1,0:T(8,128)(2,1)} %get-tuple-element.7.b, f32[24,1408]{1,0:T(8,128)} %get-tuple-element.8.d), custom_call_target="tpu_custom_call" | custom-call | tf_op jit(solution)/shard_map/pallas_call | solution.py:723

commit v6 on v5

--- a/solution.py
+++ b/solution.py
@@ -46,8 +46,8 @@
 
 
 def kernel(
-    factor, cap, tokens, widen, narrow_t, head_t, rows, owner_of, token_of, feats_out, error_out, grad,
-    feats, error, xs, w1, w2, hid, nar, nar_in, heads, head, kept, pp_out, pp_in, pc_out, pc_in, py_out, py_in, summed,
+    factor, cap, tokens, widen, narrow_in, head_t, rows_in, owner_of, token_of, feats_out, error_out, grad,
+    narrow_t, rows, feats, error, xs, w1, w2, hid, nar, nar_in, heads, head, kept, pp_out, pp_in, pc_out, pc_in, py_out, py_in, summed,
     buf_x, buf_z, mid_x, mid_z, rcv, pred, slot_of, flags, flags_in, pair_out, pair_in, shares, r1, r_own, r2, fin, gout,
     s_xp, r_xp, s_xy, r_xy, s_xf, r_xf, s_wp, r_wp, s_wx, r_wx, s_wz, r_wz,
     s_np, r_np, s_nx, r_nx, s_nz, r_nz, s_hx, r_hx, s_hz, r_hz, s_hp, r_hp,
@@ -104,7 +104,10 @@
     for other in others:
         pl.semaphore_signal(barrier, inc=1, device_id=other, device_id_type=MESH)
 
+    pltpu.make_async_copy(narrow_in, narrow_t, s_o.at[5]).start()
+    pltpu.make_async_copy(rows_in, rows, s_o.at[6]).start()
     xs[0] = norm_rows(tokens[...].astype(F32)).astype(BF16)
+    pltpu.make_async_copy(narrow_in, narrow_t, s_o.at[5]).wait()
     for core in range(2):
         for k in range(4):
             unit = (8 * core + 2 * k + p) * 384
@@ -420,6 +423,8 @@
         both = [heads[k // 4, k % 4, core, :88, :].astype(F32) for core in range(2)]
         head[k] = jnp.concatenate(both, axis=0).astype(BF16)
 
+    pltpu.make_async_copy(rows_in, rows, s_o.at[6]).wait()
+
     def predict(i, _):
         rows_at = pl.ds(pl.multiple_of(i * 128, 128), 128)
         pred[rows_at, :] = lax.dot_general(
@@ -638,7 +643,7 @@
     owners = lax.axis_size("tgt") * lax.axis_size("fsdp")
     cap, half = slots // owners, 768
     dma = pltpu.SemaphoreType.DMA
-    vmem = pl.BlockSpec(memory_space=pltpu.VMEM)
+    vmem, hbm = pl.BlockSpec(memory_space=pltpu.VMEM), pl.BlockSpec(memory_space=pl.ANY)
     part = pltpu.VMEM((2, count, half), BF16)
     return pl.pallas_call(
         functools.partial(kernel, factor, cap),
@@ -647,9 +652,11 @@
             jax.ShapeDtypeStruct((slots, width), BF16),
             jax.ShapeDtypeStruct((depth // lax.axis_size("fsdp"), width), F32),
         ),
-        in_specs=[vmem] * 7,
+        in_specs=[vmem, vmem, hbm, vmem, hbm, vmem, vmem],
         out_specs=(pl.BlockSpec(memory_space=pl.ANY), pl.BlockSpec(memory_space=pl.ANY), vmem),
         scratch_shapes=[
+            pltpu.VMEM((88, narrow_weight.shape[0]), BF16),
+            pltpu.VMEM((slots, depth), BF16),
             pltpu.VMEM((count, width), BF16),
             pltpu.VMEM((slots, 2 * half), BF16),
             pltpu.VMEM((4, count, width), BF16),
@@ -686,7 +693,7 @@
             dma((2,)), dma((2,)), dma((2,)), dma((2,)), dma((2,)), dma((2,)),
             dma((2,)), dma((2,)), dma((2,)), dma((2,)), dma((2,)), dma((2,)), dma((2,)), dma((2,)),
             dma((4,)), dma((4,)), dma((4,)), dma((4,)), dma((8,)), dma((8,)), dma((8,)), dma((8,)),
-            dma((8,)), dma((8,)), dma((4,)), dma((4,)), dma((5,)),
+            dma((8,)), dma((8,)), dma((4,)), dma((4,)), dma((7,)),
             dma, dma, dma((8,)), dma((8,)), dma((8,)), dma((8,)), dma((16,)), dma((11,)),
         ],
         compiler_params=pltpu.CompilerParams(
@@ -717,15 +724,16 @@
 
 def move(a, b, d):
     wide = a.shape[1]
-    first = pl.BlockSpec((a.shape[0] // 4, wide), lambda i: (i, 0))
-    second = pl.BlockSpec((b.shape[0] // 4, wide), lambda i: (i, 0))
+    first = pl.BlockSpec((a.shape[0] // 2, wide), lambda i: (i, 0))
+    second = pl.BlockSpec((b.shape[0] // 2, wide), lambda i: (i, 0))
     third = pl.BlockSpec(d.shape, lambda i: (0, 0))
     return pl.pallas_call(
         move_kernel,
-        grid=(4,),
+        grid=(2,),
         out_shape=tuple(jax.ShapeDtypeStruct(o.shape, o.dtype) for o in (a, b, d)),
         in_specs=[first, second, third],
         out_specs=(first, second, third),
+        compiler_params=pltpu.CompilerParams(vmem_limit_bytes=32 << 20),
     )(a, b, d)
 
 

time: 153 us -> 153 us (level)
  local copies, waits for them, and re-layouts: 0 us -> 3.95 us
  Pallas kernels: 152 us -> 149 us
    unnamed x0 -> x6, local copies, waits for them, and re-layouts: none -> 3.95 us
    pallas_call x1, Pallas kernels: 4.66 us -> 2.12 us  [move(): pl.pallas_call(move_kernel, grid=(2,), out_shape=tuple((jax.ShapeDtypeStr...]
where the time goes in v6:
time: 153 us
  Pallas kernels  149 us (97%)
  local copies, waits for them, and re-layouts  3.95 us (3%)
    pallas_call x1, Pallas kernels, step(): pl.pallas_call(functools.partial(kernel, factor, cap), out_shape=(jax.Sha...  146 us
    unnamed x6, local copies, waits for them, and re-layouts  3.95 us

profile of v6, /device:TPU:1, one launch (start us, length us, event | category | flops | bytes accessed | tf_op | source)
XLA Modules:
  0.0 153.1 jit_solution(15529662379234715762)
XLA Ops:
  0.6 146.4 %shard_map.94 = (bf16[384,1408]{1,0:T(8,128)(2,1)}, bf16[1024,1408]{1,0:T(8,128)(2,1)}, f32[24,1408]{1,0:T(8,128)}) custom-call(bf16[384,1408]{1,0:T(8,128)(2,1)} %tokens.1, bf16[1408,384]{1,0:T(8,128)(2,1)} %widen.1, bf16[88,6144]{1,0:T(8,128)(2,1)} %bitcast.4, bf16[88,384]{1,0:T(8,128)(2,1)} %bitcast.5, bf16[1024,384]{1,0:T(8,128)(2,1)} %rows_in.1, ...), custom_call_target="tpu_custom_call" | custom-call | tf_op jit(solution)/shard_map/pallas_call | solution.py:648
  147.1 0.0 copy-start
  147.1 1.8 %copy-done = bf16[1024,1408]{1,0:T(8,128)(2,1)S(1)} copy-done((bf16[1024,1408]{1,0:T(8,128)(2,1)S(1)}, bf16[1024,1408]{1,0:T(8,128)(2,1)}, u32[]{:S(2)}) %copy-start) | copy-done | bytes 2883608
  148.9 0.0 copy-start.1
  148.9 1.2 copy-done.1
  150.1 0.0 copy-start.2
  150.1 0.9 copy-done.2
  151.0 2.1 %shard_map.95 = (bf16[384,1408]{1,0:T(8,128)(2,1)}, bf16[1024,1408]{1,0:T(8,128)(2,1)}, f32[24,1408]{1,0:T(8,128)}) custom-call(bf16[384,1408]{1,0:T(8,128)(2,1)S(1)} %copy-done.1, bf16[1024,1408]{1,0:T(8,128)(2,1)S(1)} %copy-done, f32[24,1408]{1,0:T(8,128)S(1)} %copy-done.2), custom_call_target="tpu_custom_call" | custom-call | tf_op jit(solution)/shard_map/pallas_call | solution.py:730
Async XLA Ops:
  147.1 1.8 %copy-start = (bf16[1024,1408]{1,0:T(8,128)(2,1)S(1)}, bf16[1024,1408]{1,0:T(8,128)(2,1)}, u32[]{:S(2)}) copy-start(bf16[1024,1408]{1,0:T(8,128)(2,1)} %get-tuple-element.7.b) | copy-start | bytes 8650756
  148.9 1.2 copy-start.1
  150.1 0.9 copy-start.2
